TPU v7x, 32 devices: a whole 2x2x4 slice. The times are simulated.
32 devices in a mesh: segment: 4 (over y, x), seq: 8 (over z, core).
Axes of the slice: x: 2, y: 2, z: 4, core: 2. Of those that a mesh axis runs over, the one named last changes fastest.
Arguments:
- sr_tokens: bfloat16 [8192, 2048], P('seq'), may hold values from -6 to 6
- base_latent: bfloat16 [512, 2048], P('seq'), may hold values from -6 to 6
- upsample_map: int32 [8192], P('seq'), may hold values from 0 to 511, as said below
- norm_gain: float32 [2048], replicated, may hold values from 0.1 to 1.9
- w_qkv: bfloat16 [3, 2048, 2048], P(None, None, 'segment'), may hold values from -0.125 to 0.125
- qk_gain: float32 [2, 2048], P(None, 'segment'), may hold values from 0.42 to 10.4
- w_out: bfloat16 [2048, 2048], P('segment'), may hold values from -0.5 to 0.5
- block_lists: int32 [128, 8], replicated, may hold values from 0 to 127, as said below
- block_counts: int32 [128], replicated, may hold values from 1 to 8
Outputs:
- updated: bfloat16 [8192, 2048], P('seq', 'segment')
Inputs may be any that keep to these rules, and one draw needn't show every extreme that they name: upsample_map[t] names a low-resolution token whose frame, index // 64, differs by at most one from t // 1024. block_lists[b, 0] = b, and the entries of one row are distinct.
All inputs are finite; a program needn't handle non-finite values.
Results may differ from a plain program's by a relative error of at most 0.012.
The roundings to bfloat16 on the way count: a program that leaves them out, or rounds other values in their place, can miss the bound.
Values may be sent and summed in bfloat16 or wider, within the bound.
A program may use at most 128 MiB of HBM per device.

v0:
```python
import jax
import jax.numpy as jnp
from jax import lax
from jax.sharding import PartitionSpec as P

HD = 128
BASE_FT = 64
BLOCK = 64


EPSILON = 1e-06


def padded_2(x, sides, width):
    for axis, dim in sides:
        count, length = (lax.axis_size(axis), x.shape[dim])
        up = [(i, (i + 1) % count) for i in range(count - 1)]
        down = [(j, i) for i, j in up]
        last = lax.slice_in_dim(x, length - width, length, axis=dim)
        leading = lax.slice_in_dim(x, 0, width, axis=dim)
        before = lax.ppermute(last, axis, up)
        after = lax.ppermute(leading, axis, down)
        x = jnp.concatenate([before, x, after], axis=dim)
    return x


def from_partner(x, axis, stride):
    return lax.ppermute(x, axis, [(i, i ^ 1 << stride) for i in range(lax.axis_size(axis))])


def rms_scale(tensor):
    return lax.rsqrt(jnp.mean(tensor * tensor, axis=-1, keepdims=True) + EPSILON)


def block_attend(query_blocks, key_rows, value_rows, lists_here, counts_here):
    head_dim = key_rows.shape[-1]
    key_blocks = key_rows.reshape(-1, BLOCK, head_dim)[lists_here]
    value_blocks = value_rows.reshape(-1, BLOCK, head_dim)[lists_here]
    scores = jnp.einsum(
        "qbd,qwkd->qbwk", query_blocks, key_blocks, preferred_element_type=jnp.float32
    ) * head_dim ** (-0.5)
    allowed = jnp.arange(lists_here.shape[1], dtype=jnp.int32)[None, :] < counts_here[:, None]
    scores = jnp.where(allowed[:, None, :, None], scores, -jnp.inf)
    row_top = jnp.max(scores, axis=(2, 3), keepdims=True)
    weights = jnp.exp(scores - row_top)
    row_total = jnp.sum(weights, axis=(2, 3))
    prob_rows = weights.astype(jnp.bfloat16)
    summed = jnp.einsum(
        "qbwk,qwkd->qbd", prob_rows, value_blocks, preferred_element_type=jnp.float32
    )
    return (summed / row_total[:, :, None]).astype(jnp.bfloat16)


def on_device(
    sr_tokens,
    base_latent,
    upsample_map,
    norm_gain,
    w_qkv,
    qk_gain,
    w_out,
    block_lists,
    block_counts,
):
    seq_count = lax.axis_size("seq")
    seq_rank = lax.axis_index("seq")
    tok_rows = sr_tokens.shape[0]
    heads_here = w_qkv.shape[2] // HD
    groups = seq_count // heads_here
    part_rows = tok_rows // groups
    my_part = seq_rank % groups
    padded = padded_2(base_latent, (("seq", 0),), BASE_FT)
    first_row = seq_rank * base_latent.shape[0] - BASE_FT
    condition = padded[upsample_map - first_row]
    mixed_rows = sr_tokens.astype(jnp.float32) + condition.astype(jnp.float32)
    normed = (mixed_rows * rms_scale(mixed_rows) * norm_gain).astype(jnp.bfloat16)
    qk_gains = qk_gain.reshape(2, heads_here, HD)
    raw_q = jnp.dot(normed, w_qkv[0], preferred_element_type=jnp.float32).reshape(
        tok_rows, heads_here, HD
    )
    raw_k = jnp.dot(normed, w_qkv[1], preferred_element_type=jnp.float32).reshape(
        tok_rows, heads_here, HD
    )
    raw_v = jnp.dot(normed, w_qkv[2], preferred_element_type=jnp.float32).reshape(
        tok_rows, heads_here, HD
    )
    query_heads = (raw_q * rms_scale(raw_q) * qk_gains[0]).astype(jnp.bfloat16)
    key_heads = (raw_k * rms_scale(raw_k) * qk_gains[1]).astype(jnp.bfloat16)
    value_heads = raw_v.astype(jnp.bfloat16)

    def by_part(tensor):
        return (
            tensor.reshape(groups, part_rows, heads_here, HD)
            .transpose(1, 2, 0, 3)
            .reshape(part_rows, seq_count, HD)
        )

    query_recv, key_part, value_part = (
        lax.all_to_all(by_part(query_heads), "seq", split_axis=1, concat_axis=0, tiled=True),
        lax.all_to_all(by_part(key_heads), "seq", split_axis=1, concat_axis=0, tiled=True),
        lax.all_to_all(by_part(value_heads), "seq", split_axis=1, concat_axis=0, tiled=True),
    )
    key_cur = key_part.reshape(seq_count, 1, part_rows, HD)
    value_cur = value_part.reshape(seq_count, 1, part_rows, HD)
    for bit_index in range(groups.bit_length() - 1):
        key_other, value_other = from_partner((key_cur, value_cur), "seq", bit_index)
        upper_half = my_part // 2**bit_index % 2 == 1
        key_cur = jnp.where(
            upper_half,
            jnp.concatenate((key_other, key_cur), axis=1),
            jnp.concatenate((key_cur, key_other), axis=1),
        )
        value_cur = jnp.where(
            upper_half,
            jnp.concatenate((value_other, value_cur), axis=1),
            jnp.concatenate((value_cur, value_other), axis=1),
        )
    key_all = key_cur.reshape(-1, HD)
    value_all = value_cur.reshape(-1, HD)
    blocks_source = tok_rows // BLOCK
    blocks_part = part_rows // BLOCK
    block_ids = (
        jnp.arange(seq_count, dtype=jnp.int32)[:, None] * blocks_source
        + my_part * blocks_part
        + jnp.arange(blocks_part, dtype=jnp.int32)[None, :]
    ).reshape(-1)
    query_blocks = query_recv.reshape(-1, BLOCK, HD)
    attended = block_attend(
        query_blocks, key_all, value_all, block_lists[block_ids], block_counts[block_ids]
    )
    returned = lax.all_to_all(
        attended.reshape(seq_count * part_rows, 1, HD),
        "seq",
        split_axis=0,
        concat_axis=1,
        tiled=True,
    )
    local_heads = (
        returned.reshape(part_rows, heads_here, groups, HD)
        .transpose(2, 0, 1, 3)
        .reshape(tok_rows, heads_here * HD)
    )
    projected = jnp.dot(local_heads, w_out, preferred_element_type=jnp.float32)
    summed_share = lax.psum_scatter(
        projected.astype(jnp.bfloat16), "segment", scatter_dimension=1, tiled=True
    ).astype(jnp.float32)
    share_width = summed_share.shape[1]
    residual = lax.dynamic_slice_in_dim(
        mixed_rows, lax.axis_index("segment") * share_width, share_width, 1
    )
    return (residual + summed_share).astype(jnp.bfloat16)


def solution(mesh):
    placed = (
        P("seq", None),
        P("seq", None),
        P("seq"),
        P(),
        P(None, None, "segment"),
        P(None, "segment"),
        P("segment", None),
        P(),
        P(),
    )
    return jax.shard_map(
        on_device, mesh=mesh, in_specs=placed, out_specs=P("seq", "segment"), check_vma=False
    )
```

profile of v0, /device:TPU:0, one launch (start us, length us, event | category | flops | bytes accessed | tf_op | source)
XLA Modules:
  0.0 296.1 jit_solution(13565334207020749881)
XLA Ops:
  6.5 2.5 collective-permute-start
  10.3 5.6 %slice_bitcast_fusion.1 = (bf16[512,2048]{0,1:T(8,128)(2,1)}, bf16[512,2048]{0,1:T(8,128)(2,1)}, bf16[512,2048]{0,1:T(8,128)(2,1)}) fusion(bf16[3,2048,512]{2,1,0:T(8,128)(2,1)} %param.13), kind=kLoop, calls=%fused_computation.28 | loop fusion | bytes 12582912 | tf_op jit(solution)/shard_map/dot_general | solution.py:81
  16.0 4.0 %copy.34 = bf16[512,2048]{1,0:T(8,128)(2,1)} copy(bf16[512,2048]{0,1:T(8,128)(2,1)} %get-tuple-element.7) | data formatting | bytes 4194304 | tf_op jit(solution)/shard_map/dot_general | solution.py:81
  21.0 6.0 %gather_fusion = bf16[1024,2048]{1,0:T(8,128)(2,1)} fusion(bf16[192,2048]{1,0:T(8,128)(2,1)S(1)} %pad_maximum_fusion, s32[1024]{0:T(1024)S(1)} %fusion.15), kind=kCustom, calls=%fused_computation | custom fusion | bytes 8392704 | tf_op jit(solution)/shard_map/gather | solution.py:74
  27.1 8.1 %convert_add_fusion = (f32[1024,2048]{1,0:T(8,128)}, f32[1024]{0:T(1024)S(1)}) fusion(bf16[1024,2048]{1,0:T(8,128)(2,1)} %gather_fusion, bf16[1024,2048]{1,0:T(8,128)(2,1)} %param.9), kind=kLoop, calls=%fused_computation.16 | loop fusion | flops 10484736 | bytes 16781312 | tf_op jit(solution)/shard_map/add | solution.py:75
  35.2 2.7 fusion.9
  38.0 2.8 multiply_reduce_fusion.1
  40.8 1.5 multiply_convert_fusion.1
  42.3 8.2 %all-to-all-start.1 = ((bf16[512,8,128]{2,0,1:T(8,128)(2,1)}), bf16[512,8,128]{2,0,1:T(8,128)(2,1)S(1)}, u32[]{:S(2)}, u32[]{:S(2)}) async-start(bf16[512,8,128]{2,0,1:T(8,128)(2,1)} %bitcast.100), calls=%async_computation.1 | async-start | bytes 2097152 | tf_op jit(solution)/shard_map/all_to_all | solution.py:100
  50.5 4.0 %copy.36 = bf16[512,2048]{1,0:T(8,128)(2,1)} copy(bf16[512,2048]{0,1:T(8,128)(2,1)} %get-tuple-element.9) | data formatting | bytes 4194304 | tf_op jit(solution)/shard_map/dot_general | solution.py:84
  54.5 6.2 %convolution_convert_fusion.1 = bf16[1024,4,128]{2,0,1:T(8,128)(2,1)} fusion(bf16[1024,2048,1]{1,0,2:T(8,128)(2,1)} %copy-done.5, bf16[4,128,2048]{2,1,0:T(8,128)(2,1)} %bitcast.103), kind=kOutput, calls=%fused_computation.32 | convolution fusion | flops 2148007936 | bytes 7340032 | tf_op jit(solution)/shard_map/dot_general | solution.py:84
  60.7 16.4 %all-to-all-done.1 = bf16[512,8,128]{2,0,1:T(8,128)(2,1)S(1)} async-done(((bf16[512,8,128]{2,0,1:T(8,128)(2,1)}), bf16[512,8,128]{2,0,1:T(8,128)(2,1)S(1)}, u32[]{:S(2)}, u32[]{:S(2)}) %all-to-all-start.1) | async-done | bytes 1048608 | tf_op jit(solution)/shard_map/all_to_all | solution.py:100
  77.1 4.4 %all-to-all-start.2 = ((bf16[512,8,128]{2,0,1:T(8,128)(2,1)}), bf16[512,8,128]{2,0,1:T(8,128)(2,1)}, u32[]{:S(2)}, u32[]{:S(2)}) async-start(bf16[512,8,128]{2,0,1:T(8,128)(2,1)} %bitcast.105), calls=%async_computation.2 | async-start | bytes 2097152 | tf_op jit(solution)/shard_map/all_to_all | solution.py:101
  81.5 4.0 %copy.33 = bf16[512,2048]{1,0:T(8,128)(2,1)} copy(bf16[512,2048]{0,1:T(8,128)(2,1)} %get-tuple-element.8) | data formatting | bytes 4194304 | tf_op jit(solution)/shard_map/dot_general | solution.py:78
  85.5 5.3 %multiply_reduce_fusion.2 = (f32[1024,4]{0,1:T(4,128)S(1)}, f32[1024,4,128]{2,0,1:T(8,128)S(1)}) fusion(bf16[1024,2048,1]{1,0,2:T(8,128)(2,1)} %copy-done.5, bf16[4,128,2048]{2,1,0:T(8,128)(2,1)} %bitcast.102), kind=kOutput, calls=%fused_computation.30 | convolution fusion | flops 2148528128 | bytes 8404992 | tf_op jit(solution)/shard_map/dot_general | solution.py:78
  90.9 1.5 multiply_convert_fusion.2
  92.4 15.5 %all-to-all-done.2 = bf16[512,8,128]{2,0,1:T(8,128)(2,1)} async-done(((bf16[512,8,128]{2,0,1:T(8,128)(2,1)}), bf16[512,8,128]{2,0,1:T(8,128)(2,1)}, u32[]{:S(2)}, u32[]{:S(2)}) %all-to-all-start.2) | async-done | bytes 1048608 | tf_op jit(solution)/shard_map/all_to_all | solution.py:101
  108.0 3.6 %all-to-all-start = ((bf16[512,8,128]{2,0,1:T(8,128)(2,1)}), bf16[512,8,128]{2,0,1:T(8,128)(2,1)S(1)}, u32[]{:S(2)}, u32[]{:S(2)}) async-start(bf16[512,8,128]{2,0,1:T(8,128)(2,1)} %bitcast.99), calls=%async_computation | async-start | bytes 2097152 | tf_op jit(solution)/shard_map/all_to_all | solution.py:99
  114.7 1.5 collective-permute-done.3
  116.2 5.7 %maximum_select_fusion = (bf16[8,2,512,128]{3,2,1,0:T(8,128)(2,1)}, bf16[8,2,512,128]{3,2,1,0:T(8,128)(2,1)}) fusion(bf16[8,1,512,128]{3,2,1,0:T(8,128)(2,1)} %bitcast.97, bf16[8,1,512,128]{3,2,1,0:T(8,128)(2,1)} %collective-permute-done.2, pred[]{:T(512)S(6)} %eq.6, bf16[8,1,512,128]{3,2,1,0:T(8,128)(2,1)} %collective-permute-done.3, ...), kind=kLoop, calls=%fused_computation.20 | loop fusion | flops 6291456 | bytes 8388609 | tf_op jit(solution)/shard_map/jit(_where)/select_n | solution.py:108
  121.9 21.2 %gather_fusion.3 = bf16[512,64,128]{2,1,0:T(8,128)(2,1)} fusion(bf16[128,64,128]{2,1,0:T(8,128)(2,1)} %bitcast.93, s32[1024]{0:T(1024)S(1)} %pad_clamp_fusion), kind=kCustom, calls=%fused_computation.3 | custom fusion | bytes 16779264 | tf_op jit(solution)/shard_map/gather | solution.py:37
  143.1 21.5 %gather_fusion.4 = bf16[512,64,128]{2,1,0:T(8,128)(2,1)} fusion(bf16[128,64,128]{2,1,0:T(8,128)(2,1)} %bitcast.92, s32[1024]{0:T(1024)S(1)} %pad_clamp_fusion), kind=kCustom, calls=%fused_computation.4 | custom fusion | bytes 16779264 | tf_op jit(solution)/shard_map/gather | solution.py:38
  164.6 5.7 %fusion = (f32[64,64]{1,0:T(8,128)S(1)}, f32[64,64,8,64]{1,3,2,0:T(8,128)S(1)}) fusion(pred[64,8]{1,0:T(8,128)(4,1)S(1)} %iota_compare_fusion, bf16[64,64,128,1]{2,1,3,0:T(8,128)(2,1)S(1)} %bitcast.94, bf16[64,8,64,128]{3,2,1,0:T(8,128)(2,1)} %bitcast.91), kind=kOutput, calls=%fused_computation.7 | convolution fusion | flops 543158272 | bytes 17842688 | tf_op jit(solution)/shard_map/qbd,qwkd->qbwk/dot_general | solution.py:39
  170.3 4.3 %fusion.1 = f32[64,64]{1,0:T(8,128)S(1)} fusion(f32[64,64,8,64]{1,3,2,0:T(8,128)S(1)} %get-tuple-element.17, f32[64,64]{1,0:T(8,128)S(1)} %get-tuple-element.16, pred[64,8]{1,0:T(8,128)(4,1)S(1)} %iota_compare_fusion), kind=kLoop, calls=%fused_computation.8 | loop fusion | flops 8384512 | bytes 8421888 | tf_op jit(solution)/shard_map/reduce_sum | solution.py:46
  176.1 12.0 %fusion.10 = bf16[64,64,128]{2,1,0:T(8,128)(2,1)} fusion(bf16[64,8,64,128]{3,2,1,0:T(8,128)(2,1)} %bitcast.95, f32[64,64,8,64]{1,3,2,0:T(8,128)} %copy-done.2, f32[64,64]{1,0:T(8,128)S(1)} %get-tuple-element.16, pred[64,8]{1,0:T(8,128)(4,1)S(1)} %iota_compare_fusion, f32[64,64]{1,0:T(8,128)S(1)} %fusion.1), kind=kOutput, calls=%fused_computation.23 | convolution fusion | flops 546308096 | bytes 17859072 | tf_op jit(solution)/shard_map/qbwk,qwkd->qbd/dot_general | solution.py:48
  188.6 2.7 reduce
  192.4 31.5 %all_to_all.60 = bf16[8,2,32768]{2,1,0:T(2,128)(2,1)S(1)} all-to-all(bf16[8,2,32768]{2,1,0:T(2,128)(2,1)} %reshape.214), channel_id=1, replica_groups=mesh['segment'=4,'seq'=8] {'seq'}, dimensions={0} | all-to-all | bytes 2097152 | tf_op jit(solution)/shard_map/all_to_all | solution.py:131
  223.9 3.5 %reshape.215 = bf16[4096,1,128]{2,1,0:T(2,128)(2,1)} reshape(bf16[8,2,32768]{2,1,0:T(2,128)(2,1)S(1)} %all_to_all.60) | data formatting | bytes 2097152
  227.4 1.7 copy.43
  230.0 4.3 %convolution_convert_fusion = bf16[1024,2048]{1,0:T(8,128)(2,1)} fusion(bf16[512,2048]{1,0:T(8,128)(2,1)S(1)} %copy-done, bf16[128,8,4,128]{3,2,1,0:T(4,128)(2,1)S(1)} %bitcast.106), kind=kOutput, calls=%fused_computation.19 | convolution fusion | flops 2149580800 | bytes 7340032 | tf_op jit(solution)/shard_map/dot_general | solution.py:143
  234.3 51.7 %reduce-scatter.2.cloned.1.call-done = bf16[1024,512]{1,0:T(8,128)(2,1)} async-done(((bf16[1024,2048]{1,0:T(8,128)(2,1)}), bf16[1024,512]{1,0:T(8,128)(2,1)}) %reduce-scatter.2.cloned.1.call-update) | async-done | bytes 1048592 | tf_op jit(solution)/shard_map/reduce_scatter | solution.py:144
  286.0 3.2 %add_convert_fusion = bf16[1024,512]{1,0:T(8,128)(2,1)} fusion(bf16[1024,512]{1,0:T(8,128)(2,1)} %reduce-scatter.2.cloned.1.call-done, f32[1024,2048]{1,0:T(8,128)} %get-tuple-element.5, s32[]{:T(128)S(6)} %select_n.66), kind=kLoop, calls=%fused_computation.24 | loop fusion | flops 1572864 | bytes 4194308 | tf_op jit(solution)/shard_map/convert_element_type | solution.py:151
  (56 shorter events, 9.4 us)
Async XLA Ops:
  6.5 223.4 %copy-start = (bf16[512,2048]{1,0:T(8,128)(2,1)S(1)}, bf16[512,2048]{1,0:T(8,128)(2,1)}, u32[]{:S(2)}) copy-start(bf16[512,2048]{1,0:T(8,128)(2,1)} %param.15) | copy-start | bytes 6291460
  6.5 9.4 %copy-start.11 = (f32[2,512]{1,0:T(2,128)S(1)}, f32[2,512]{1,0:T(2,128)}, u32[]{:S(2)}) copy-start(f32[2,512]{1,0:T(2,128)} %param.14) | copy-start | bytes 12292
  6.5 13.5 %collective-permute-start = (bf16[64,2048]{1,0:T(8,128)(2,1)}, bf16[64,2048]{1,0:T(8,128)(2,1)S(1)}, u32[]{:S(2)}, u32[]{:S(2)}) collective-permute-start(bf16[64,2048]{1,0:T(8,128)(2,1)} %param.10), channel_id=1, source_target_pairs={{0,1},{1,2},{2,3},{3,4},{4,5},{5,6},{6,7},{8,9},{9,10},{10,11},{11... | collective-permute-start | bytes 786440 | tf_op jit(solution)/shard_map/ppermute | solution.py:21
  9.0 11.0 %collective-permute-start.1 = (bf16[64,2048]{1,0:T(8,128)(2,1)}, bf16[64,2048]{1,0:T(8,128)(2,1)}, u32[]{:S(2)}, u32[]{:S(2)}) collective-permute-start(bf16[64,2048]{1,0:T(8,128)(2,1)} %param.10), channel_id=1, source_target_pairs={{1,0},{2,1},{3,2},{4,3},{5,4},{6,5},{7,6},{9,8},{10,9},{11,10},{12... | collective-permute-start | bytes 786440 | tf_op jit(solution)/shard_map/ppermute | solution.py:22
  16.0 4.0 %copy-start.12 = (s32[1024]{0:T(1024)S(1)}, s32[1024]{0:T(1024)}, u32[]{:S(2)}) copy-start(s32[1024]{0:T(1024)} %param.11) | copy-start | bytes 12292
  16.0 4.1 %copy-start.8 = (bf16[64,2048]{1,0:T(8,128)(2,1)S(1)}, bf16[64,2048]{1,0:T(8,128)(2,1)}, u32[]{:S(2)}) copy-start(bf16[64,2048]{1,0:T(8,128)(2,1)} %param.10) | copy-start | bytes 786436
  27.1 8.2 %copy-start.3 = (bf16[1024,2048]{1,0:T(8,128)(2,1)S(1)}, bf16[1024,2048]{1,0:T(8,128)(2,1)}, u32[]{:S(2)}) copy-start(bf16[1024,2048]{1,0:T(8,128)(2,1)} %gather_fusion) | copy-start | bytes 12582916
  27.1 8.2 %copy-start.4 = (bf16[1024,2048]{1,0:T(8,128)(2,1)S(1)}, bf16[1024,2048]{1,0:T(8,128)(2,1)}, u32[]{:S(2)}) copy-start(bf16[1024,2048]{1,0:T(8,128)(2,1)} %param.9) | copy-start | bytes 12582916
  27.1 8.2 %copy-start.9 = (f32[2048]{0:T(1024)S(1)}, f32[2048]{0:T(1024)}, u32[]{:S(2)}) copy-start(f32[2048]{0:T(1024)} %param.12) | copy-start | bytes 24580
  35.2 2.8 copy-start.7
  38.0 2.8 copy-start.5
  42.3 34.8 %all-to-all-start.1 = ((bf16[512,8,128]{2,0,1:T(8,128)(2,1)}), bf16[512,8,128]{2,0,1:T(8,128)(2,1)S(1)}, u32[]{:S(2)}, u32[]{:S(2)}) async-start(bf16[512,8,128]{2,0,1:T(8,128)(2,1)} %bitcast.100), calls=%async_computation.1 | async-start | bytes 2097152 | tf_op jit(solution)/shard_map/all_to_all | solution.py:100
  77.1 8.4 %copy-start.6 = (bf16[512,8,128]{2,0,1:T(8,128)(2,1)}, bf16[512,8,128]{2,0,1:T(8,128)(2,1)S(1)}, u32[]{:S(2)}) copy-start(bf16[512,8,128]{2,0,1:T(8,128)(2,1)S(1)} %all-to-all-done.1) | copy-start | bytes 3145732
  77.1 30.8 %all-to-all-start.2 = ((bf16[512,8,128]{2,0,1:T(8,128)(2,1)}), bf16[512,8,128]{2,0,1:T(8,128)(2,1)}, u32[]{:S(2)}, u32[]{:S(2)}) async-start(bf16[512,8,128]{2,0,1:T(8,128)(2,1)} %bitcast.105), calls=%async_computation.2 | async-start | bytes 2097152 | tf_op jit(solution)/shard_map/all_to_all | solution.py:101
  90.8 21.5 %copy-start.10 = (s32[128,8]{0,1:T(8,128)S(1)}, s32[128,8]{0,1:T(8,128)}, u32[]{:S(2)}) copy-start(s32[128,8]{0,1:T(8,128)} %param.16) | copy-start | bytes 12292
  90.8 22.3 %copy-start.1 = (s32[128]{0:T(128)S(1)}, s32[128]{0:T(128)}, u32[]{:S(2)}) copy-start(s32[128]{0:T(128)} %param.17) | copy-start | bytes 1540
  108.0 56.6 %all-to-all-start = ((bf16[512,8,128]{2,0,1:T(8,128)(2,1)}), bf16[512,8,128]{2,0,1:T(8,128)(2,1)S(1)}, u32[]{:S(2)}, u32[]{:S(2)}) async-start(bf16[512,8,128]{2,0,1:T(8,128)(2,1)} %bitcast.99), calls=%async_computation | async-start | bytes 2097152 | tf_op jit(solution)/shard_map/all_to_all | solution.py:99
  111.5 174.5 %reduce-scatter.2.cloned.1.call-start = ((), (), s32[]{:S(2)}) async-start(), calls=%async_computation.5 | async-start | bytes 5242880 | tf_op jit(solution)/shard_map/reduce_scatter | solution.py:144
  111.6 3.1 %collective-permute-start.2 = (bf16[8,1,512,128]{3,2,1,0:T(8,128)(2,1)}, bf16[8,1,512,128]{3,2,1,0:T(8,128)(2,1)}, u32[]{:S(2)}, u32[]{:S(2)}) collective-permute-start(bf16[8,1,512,128]{3,2,1,0:T(8,128)(2,1)} %bitcast.96), channel_id=1, source_target_pairs={{0,1},{1,0},{2,3},{3,2},{4,5},{5,4},{6,7},{7,6},{8,9},{9,8},{10,11... | collective-permute-start | bytes 3145736 | tf_op jit(solution)/shard_map/ppermute | solution.py:28
  112.0 4.2 %collective-permute-start.3 = (bf16[8,1,512,128]{3,2,1,0:T(8,128)(2,1)}, bf16[8,1,512,128]{3,2,1,0:T(8,128)(2,1)}, u32[]{:S(2)}, u32[]{:S(2)}) collective-permute-start(bf16[8,1,512,128]{3,2,1,0:T(8,128)(2,1)} %bitcast.37), channel_id=1, source_target_pairs={{0,1},{1,0},{2,3},{3,2},{4,5},{5,4},{6,7},{7,6},{8,9},{9,8},{10,11... | collective-permute-start | bytes 3145736 | tf_op jit(solution)/shard_map/ppermute | solution.py:28
  170.3 5.7 %copy-start.2 = (f32[64,64,8,64]{1,3,2,0:T(8,128)}, f32[64,64,8,64]{1,3,2,0:T(8,128)S(1)}, u32[]{:S(2)}) copy-start(f32[64,64,8,64]{1,3,2,0:T(8,128)S(1)} %get-tuple-element.17) | copy-start | bytes 25165828
Sparse Core Ops, SparseCore 0:
  234.4 51.5 reduce-scatter.1
where the time goes:
time: 297 us; the launch traced here: 296 us
  waiting for transfers between devices  85.8 us (29%)
  local copies, waits for them, and re-layouts  77 us (26%)
  matrix products  36.3 us (12%)
  blocking collectives  31.5 us (11%)
  other arithmetic  31 us (10%)
  starting transfers between devices  20.6 us (7%)
  between operations  13.7 us (5%)
    reduce_scatter x1, waiting for transfers between devices, on_device(): lax.psum_scatter(projected.astype(jnp.bfloat16), 'segment', scatter_dimen...  51.7 us
    all_to_all x1, blocking collectives, on_device(): lax.all_to_all(attended.reshape(seq_count * part_rows, 1, HD), 'seq', spl...  31.5 us
    gather x1, local copies, waits for them, and re-layouts, block_attend(): value_blocks = value_rows.reshape(-1, BLOCK, head_dim)[lists_here]  21.5 us
    gather x1, local copies, waits for them, and re-layouts, block_attend(): key_blocks = key_rows.reshape(-1, BLOCK, head_dim)[lists_here]  21.2 us
    all_to_all x1, waiting for transfers between devices, on_device(): lax.all_to_all(by_part(key_heads), 'seq', split_axis=1, concat_axis=0, ti...  16.4 us
    all_to_all x1, waiting for transfers between devices, on_device(): lax.all_to_all(by_part(value_heads), 'seq', split_axis=1, concat_axis=0,...  15.5 us
    dot_general x1, matrix products, block_attend(): jnp.einsum('qbwk,qwkd->qbd', prob_rows, value_blocks, preferred_element_t...  12 us
    dot_general x2, local copies, waits for them, and re-layouts, on_device(): jnp.dot(normed, w_qkv[1], preferred_element_type=jnp.float32)  9.61 us
  transfers between devices with their start and end apart: 8, of which 5 were waited for; matrix products, arithmetic and copies ran while one was open for 27% of the time, Pallas kernels for 0%

commit v1 on v0

v1 whole, which is shorter than its diff:
```python
import functools

import jax
import jax.numpy as jnp
from jax import lax
from jax.experimental import pallas as pl
from jax.experimental.pallas import tpu as pltpu
from jax.sharding import PartitionSpec as P

HD = 128
BASE_FT = 64
BLOCK = 64
EPSILON = 1e-06
CHUNKS = 4
MESH = pl.DeviceIdType.MESH
MIB = 2**20


def padded_2(x, axis, width):
    count, length = lax.axis_size(axis), x.shape[0]
    up = [(i, (i + 1) % count) for i in range(count - 1)]
    down = [(j, i) for i, j in up]
    before = lax.ppermute(lax.slice_in_dim(x, length - width, length, axis=0), axis, up)
    after = lax.ppermute(lax.slice_in_dim(x, 0, width, axis=0), axis, down)
    return jnp.concatenate([before, x, after], axis=0)


def rms_scale(tensor):
    return lax.rsqrt(jnp.mean(tensor * tensor, axis=-1, keepdims=True) + EPSILON)


def front_kernel(heads, sr, base, place, gain, w_qkv, qk_gain, q_out, kv_out, share_out, mixed):
    rows = sr.shape[0]
    count = base.shape[0]
    hot = (lax.broadcasted_iota(jnp.int32, (rows, count), 1) == place[...]).astype(jnp.bfloat16)
    condition = jnp.dot(hot, base[...], preferred_element_type=jnp.float32)
    mixed[...] = sr[...].astype(jnp.float32) + condition
    width = share_out.shape[1]
    start = pl.multiple_of(lax.axis_index("segment") * width, width)
    share_out[...] = mixed[:, pl.ds(start, width)]
    whole = mixed[...]
    normed = (whole * rms_scale(whole) * gain[...]).astype(jnp.bfloat16)
    for which in range(3):
        raw = jnp.dot(normed, w_qkv[which], preferred_element_type=jnp.float32)
        for head in range(heads):
            cols = slice(head * HD, (head + 1) * HD)
            part = raw[:, cols]
            if which < 2:
                part = part * rms_scale(part) * qk_gain[which : which + 1, cols]
            part = part.astype(jnp.bfloat16)
            if which == 0:
                q_out[head] = part
            else:
                kv_out[head, which - 1] = part


def front(sr, base, place, gain, w_qkv, qk_gain):
    rows, depth = sr.shape
    width = w_qkv.shape[2]
    heads = width // HD
    tile = 256
    share = depth // lax.axis_size("segment")
    return pl.pallas_call(
        functools.partial(front_kernel, heads),
        grid=(rows // tile,),
        in_specs=[
            pl.BlockSpec((tile, depth), lambda i: (i, 0)),
            pl.BlockSpec(base.shape, lambda i: (0, 0)),
            pl.BlockSpec((tile, 1), lambda i: (i, 0)),
            pl.BlockSpec((1, depth), lambda i: (0, 0)),
            pl.BlockSpec(w_qkv.shape, lambda i: (0, 0, 0)),
            pl.BlockSpec(qk_gain.shape, lambda i: (0, 0)),
        ],
        out_specs=[
            pl.BlockSpec((heads, tile, HD), lambda i: (0, i, 0)),
            pl.BlockSpec((heads, 2, tile, HD), lambda i: (0, 0, i, 0)),
            pl.BlockSpec((tile, share), lambda i: (i, 0)),
        ],
        out_shape=[
            jax.ShapeDtypeStruct((heads, rows, HD), jnp.bfloat16),
            jax.ShapeDtypeStruct((heads, 2, rows, HD), jnp.bfloat16),
            jax.ShapeDtypeStruct((rows, share), jnp.float32),
        ],
        scratch_shapes=[pltpu.VMEM((tile, depth), jnp.float32)],
        compiler_params=pltpu.CompilerParams(vmem_limit_bytes=48 * MIB),
        name="front",
    )(sr, base, place, gain, w_qkv, qk_gain)


def greet(targets):
    barrier = pltpu.get_barrier_semaphore()
    for target in targets:
        pl.semaphore_signal(barrier, inc=1, device_id=target, device_id_type=MESH)
    pl.semaphore_wait(barrier, len(targets))


def remote(src, dst, send, recv, target):
    return pltpu.make_async_remote_copy(
        src_ref=src, dst_ref=dst, send_sem=send, recv_sem=recv, device_id=target, device_id_type=MESH
    )


def exchange_kernel(
    seqs, segs, groups, q, kv, w_out, kv_all, q_all, w_cols,
    kv_send, kv_recv, q_send, q_recv, fw_send, fw_recv, w_send, w_recv, own,
):
    me, seg = lax.axis_index("seq"), lax.axis_index("segment")
    rows = q.shape[1]
    part_rows = rows // groups
    head, part = me // groups, me % groups
    depth, share = w_out.shape[0], w_out.shape[1] // segs
    greet(
        [(seg, lax.rem(me + k, seqs)) for k in range(1, seqs)]
        + [(lax.rem(seg + k, segs), me) for k in range(1, segs)]
    )

    def rows_of(which):
        return pl.ds(pl.multiple_of(which * part_rows, part_rows), part_rows)

    def landing(source, which):
        start = pl.multiple_of(source * rows + which * part_rows, part_rows)
        return kv_all.at[:, pl.ds(start, part_rows), :]

    def kv_copy(target, source):
        return remote(
            kv.at[target // groups, :, rows_of(target % groups), :],
            landing(source, target % groups),
            kv_send.at[target],
            kv_recv.at[source],
            (seg, target),
        )

    def q_copy(target, source):
        return remote(
            q.at[target // groups, rows_of(target % groups), :],
            q_all.at[source],
            q_send.at[target],
            q_recv.at[source],
            (seg, target),
        )

    def w_copy(target, source):
        return remote(
            w_out.at[:, pl.ds(pl.multiple_of(target * share, share), share)],
            w_cols.at[pl.ds(pl.multiple_of(source * depth, depth), depth), :],
            w_send.at[target],
            w_recv.at[source],
            (target, me),
        )

    def forward(source, step, sender_part):
        slot = landing(source, sender_part)
        target = head * groups + lax.rem(part + step, groups)
        return remote(
            slot, slot, fw_send.at[source, step - 1], fw_recv.at[source, step - 1], (seg, target)
        )

    own_kv = pltpu.make_async_copy(kv.at[head, :, rows_of(part), :], landing(me, part), own.at[0])
    own_q = pltpu.make_async_copy(q.at[head, rows_of(part), :], q_all.at[me], own.at[1])
    own_w = pltpu.make_async_copy(
        w_out.at[:, pl.ds(pl.multiple_of(seg * share, share), share)],
        w_cols.at[pl.ds(pl.multiple_of(seg * depth, depth), depth), :],
        own.at[2],
    )
    own_kv.start()

    @pl.loop(1, seqs)
    def _(k):
        kv_copy(lax.rem(me + k, seqs), me).start()

    @pl.loop(1, seqs)
    def _(k):
        q_copy(lax.rem(me + k, seqs), me).start()

    own_q.start()
    own_w.start()

    @pl.loop(1, segs)
    def _(k):
        w_copy(lax.rem(seg + k, segs), seg).start()

    own_kv.wait()
    for step in range(1, groups):
        forward(me, step, part).start()

    @pl.loop(1, seqs)
    def _(k):
        source = lax.rem(me + seqs - k, seqs)
        kv_copy(me, source).wait_recv()
        for step in range(1, groups):
            forward(source, step, part).start()

    @pl.loop(0, seqs)
    def _(k):
        source = lax.rem(me + k, seqs)
        for step in range(1, groups):
            forward(source, step, lax.rem(part + groups - step, groups)).wait_recv()
            forward(source, step, part).wait_send()

    @pl.loop(1, seqs)
    def _(k):
        q_copy(me, lax.rem(me + seqs - k, seqs)).wait_recv()
        target = lax.rem(me + k, seqs)
        kv_copy(target, me).wait_send()
        q_copy(target, me).wait_send()

    @pl.loop(1, segs)
    def _(k):
        w_copy(seg, lax.rem(seg + segs - k, segs)).wait_recv()
        w_copy(lax.rem(seg + k, segs), seg).wait_send()

    own_q.wait()
    own_w.wait()


def exchange(q, kv, w_out, seqs, segs, groups):
    heads, rows, _ = q.shape
    depth, width = w_out.shape
    dma = pltpu.SemaphoreType.DMA
    anywhere = pl.BlockSpec(memory_space=pl.ANY)
    return pl.pallas_call(
        functools.partial(exchange_kernel, seqs, segs, groups),
        in_specs=[anywhere] * 3,
        out_specs=[anywhere] * 3,
        out_shape=[
            jax.ShapeDtypeStruct((2, seqs * rows, HD), jnp.bfloat16),
            jax.ShapeDtypeStruct((seqs, rows // groups, HD), jnp.bfloat16),
            jax.ShapeDtypeStruct((segs * depth, width // segs), jnp.bfloat16),
        ],
        scratch_shapes=[
            dma((seqs,)), dma((seqs,)), dma((seqs,)), dma((seqs,)),
            dma((seqs, max(groups - 1, 1))), dma((seqs, max(groups - 1, 1))),
            dma((segs,)), dma((segs,)), dma((3,)),
        ],
        compiler_params=pltpu.CompilerParams(collective_id=0, has_side_effects=True),
        name="exchange",
    )(q, kv, w_out)


def attend_kernel(blocks_source, blocks_part, groups, together, lists, counts, q, kv, out):
    window = lists.shape[0] // counts.shape[0]
    first = (lax.axis_index("seq") % groups) * blocks_part
    span = window * BLOCK
    column = lax.broadcasted_iota(jnp.int32, (BLOCK, span), 1)

    def one(index):
        block = (index // blocks_part) * blocks_source + first + index % blocks_part
        starts = [pl.multiple_of(lists[block * window + w] * BLOCK, BLOCK) for w in range(window)]
        keys = jnp.concatenate([kv[0, pl.ds(at, BLOCK), :] for at in starts], axis=0)
        values = jnp.concatenate([kv[1, pl.ds(at, BLOCK), :] for at in starts], axis=0)
        query = q[pl.ds(pl.multiple_of(index * BLOCK, BLOCK), BLOCK), :]
        scores = lax.dot_general(
            query, keys, (((1,), (1,)), ((), ())), preferred_element_type=jnp.float32
        ) * HD ** (-0.5)
        scores = jnp.where(column < counts[block] * BLOCK, scores, -jnp.inf)
        weights = jnp.exp(scores - jnp.max(scores, axis=1, keepdims=True))
        total = jnp.sum(weights, axis=1, keepdims=True)
        summed = jnp.dot(weights.astype(jnp.bfloat16), values, preferred_element_type=jnp.float32)
        return (summed / total).astype(jnp.bfloat16)

    @pl.loop(0, out.shape[0] // (BLOCK * together))
    def _(step):
        done = [one(step * together + i) for i in range(together)]
        for i in range(together):
            at = pl.multiple_of((step * together + i) * BLOCK, BLOCK)
            out[pl.ds(at, BLOCK), :] = done[i]


def attend(lists, counts, q, kv, blocks_source, groups):
    blocks_part = blocks_source // groups
    return pl.pallas_call(
        functools.partial(attend_kernel, blocks_source, blocks_part, groups, 4),
        in_specs=[pl.BlockSpec(memory_space=pltpu.SMEM)] * 2
        + [pl.BlockSpec(memory_space=pltpu.VMEM)] * 2,
        out_specs=pl.BlockSpec(memory_space=pltpu.VMEM),
        out_shape=jax.ShapeDtypeStruct(q.shape, jnp.bfloat16),
        compiler_params=pltpu.CompilerParams(vmem_limit_bytes=48 * MIB),
        name="attend",
    )(lists, counts, q, kv)


def finish_kernel(
    seqs, groups, chunks, att, w_cols, share, out, full, z_send, z_recv, p_send, p_recv, own,
):
    me, seg = lax.axis_index("seq"), lax.axis_index("segment")
    head, part = me // groups, me % groups
    part_rows = att.shape[1]
    size = part_rows // chunks
    half = size // 2
    width = full.shape[3]
    near_x, near_y = seg ^ 1, seg ^ 2
    greet(
        [(seg, lax.rem(me + k, seqs)) for k in range(1, seqs)] + [(near_x, me), (near_y, me)]
    )

    def spot(chunk, owner):
        lanes = pl.ds(pl.multiple_of((owner // groups) * HD, HD), HD)
        return full.at[seg, owner % groups, pl.ds(pl.multiple_of(chunk * size, size), size), lanes]

    def z_copy(chunk, target, owner):
        return remote(
            att.at[target, pl.ds(pl.multiple_of(chunk * size, size), size), :],
            spot(chunk, owner),
            z_send.at[chunk, target],
            z_recv.at[chunk, owner],
            (seg, target),
        )

    def own_copy(chunk):
        return pltpu.make_async_copy(
            att.at[me, pl.ds(pl.multiple_of(chunk * size, size), size), :],
            spot(chunk, me),
            own.at[chunk],
        )

    def pair_copy(chunk, kind, origin, to):
        at = pl.multiple_of(chunk * size + (half if kind == 3 else 0), half)
        piece = full.at[origin, :, pl.ds(at, size if kind < 2 else half), :]
        return remote(piece, piece, p_send.at[chunk, kind], p_recv.at[chunk, kind], (to, me))

    @pl.loop(0, chunks)
    def _(chunk):
        own_copy(chunk).start()

        @pl.loop(1, seqs)
        def _(k):
            z_copy(chunk, lax.rem(me + k, seqs), me).start()

    @pl.loop(0, chunks + 2)
    def _(step):
        @pl.when(step < chunks)
        def _():
            own_copy(step).wait()

            @pl.loop(1, seqs)
            def _(k):
                z_copy(step, me, lax.rem(me + seqs - k, seqs)).wait_recv()

            pair_copy(step, 0, seg, near_x).start()
            pair_copy(step, 1, seg, near_y).start()

        @pl.when(jnp.logical_and(step >= 1, step < chunks + 1))
        def _():
            chunk = step - 1
            pair_copy(chunk, 0, near_x, near_x).wait_recv()
            pair_copy(chunk, 2, near_x, near_y).start()
            pair_copy(chunk, 1, near_y, near_y).wait_recv()
            pair_copy(chunk, 3, near_y, near_x).start()

        @pl.when(step >= 2)
        def _():
            chunk = step - 2
            far = seg ^ 3
            pair_copy(chunk, 2, far, near_y).wait_recv()
            pair_copy(chunk, 3, far, near_x).wait_recv()
            rows = pl.ds(pl.multiple_of(chunk * size, size), size)
            total = jnp.zeros((groups * size, out.shape[2]), jnp.float32)
            for j in range(full.shape[0]):
                piece = full[j, :, rows, :].reshape(groups * size, width)
                total += jnp.dot(
                    piece, w_cols[j * width : (j + 1) * width, :], preferred_element_type=jnp.float32
                )
            total = total.reshape(groups, size, out.shape[2])
            out[:, rows, :] = (share[:, rows, :] + total).astype(jnp.bfloat16)

    @pl.loop(0, chunks)
    def _(chunk):
        pair_copy(chunk, 0, seg, near_x).wait_send()
        pair_copy(chunk, 1, seg, near_y).wait_send()
        pair_copy(chunk, 2, near_x, near_y).wait_send()
        pair_copy(chunk, 3, near_y, near_x).wait_send()

        @pl.loop(1, seqs)
        def _(k):
            z_copy(chunk, lax.rem(me + k, seqs), me).wait_send()


def finish(att, w_cols, share, seqs, segs, groups):
    part_rows = att.shape[1]
    width = w_cols.shape[0] // segs
    cols = w_cols.shape[1]
    dma = pltpu.SemaphoreType.DMA
    vmem = pl.BlockSpec(memory_space=pltpu.VMEM)
    return pl.pallas_call(
        functools.partial(finish_kernel, seqs, groups, CHUNKS),
        in_specs=[vmem] * 3,
        out_specs=vmem,
        out_shape=jax.ShapeDtypeStruct((groups, part_rows, cols), jnp.bfloat16),
        scratch_shapes=[
            pltpu.VMEM((segs, groups, part_rows, width), jnp.bfloat16),
            dma((CHUNKS, seqs)), dma((CHUNKS, seqs)), dma((CHUNKS, 4)), dma((CHUNKS, 4)),
            dma((CHUNKS,)),
        ],
        compiler_params=pltpu.CompilerParams(
            collective_id=1, has_side_effects=True, vmem_limit_bytes=48 * MIB
        ),
        name="finish",
    )(att, w_cols, share)


def on_device(
    sr_tokens, base_latent, upsample_map, norm_gain, w_qkv, qk_gain, w_out, block_lists, block_counts
):
    seqs, segs = lax.axis_size("seq"), lax.axis_size("segment")
    rank = lax.axis_index("seq")
    rows = sr_tokens.shape[0]
    heads = w_qkv.shape[2] // HD
    groups = seqs // heads
    part_rows = rows // groups
    padded = padded_2(base_latent, "seq", BASE_FT)
    place = (upsample_map - (rank * base_latent.shape[0] - BASE_FT))[:, None]
    q, kv, share = front(sr_tokens, padded, place, norm_gain[None], w_qkv, qk_gain)
    kv_all, q_all, w_cols = exchange(q, kv, w_out, seqs, segs, groups)
    att = attend(
        block_lists.reshape(-1), block_counts, q_all.reshape(-1, HD), kv_all, rows // BLOCK, groups
    )
    out = finish(
        att.reshape(seqs, part_rows, HD), w_cols, share.reshape(groups, part_rows, -1), seqs, segs, groups
    )
    return out.reshape(rows, -1)


def solution(mesh):
    placed = (
        P("seq", None),
        P("seq", None),
        P("seq"),
        P(),
        P(None, None, "segment"),
        P(None, "segment"),
        P("segment", None),
        P(),
        P(),
    )
    return jax.shard_map(
        on_device, mesh=mesh, in_specs=placed, out_specs=P("seq", "segment"), check_vma=False
    )
```

time: 297 us -> 178 us (0.60)
  Pallas kernels: 0 us -> 162 us
  waiting for transfers between devices: 85.8 us -> 2.7 us
  local copies, waits for them, and re-layouts: 77 us -> 5.62 us
  matrix products: 36.3 us -> 0 us
  blocking collectives: 31.5 us -> 0 us
  other arithmetic: 31 us -> 1.71 us
  starting transfers between devices: 20.6 us -> 3.79 us
  between operations: 13.7 us -> 0.11 us
    pallas_call x0 -> x4, Pallas kernels: none -> 162 us  [the longest x1 69.5 us: exchange(): pl.pallas_call(functools.partial(exchange_kernel, seqs, segs, groups), in...]
    reduce_scatter x1 -> x0, waiting for transfers between devices: 51.7 us -> none  [on_device(): lax.psum_scatter(projected.astype(jnp.bfloat16), 'segment', scatter_dimen...]
    gather x5 -> x0, local copies, waits for them, and re-layouts: 50.1 us -> none  [the longest x1 21.5 us: block_attend(): value_blocks = value_rows.reshape(-1, BLOCK, head_dim)[lists_here]]
    dot_general x6 -> x0, matrix products: 36.3 us -> none  [the longest x1 12 us: block_attend(): jnp.einsum('qbwk,qwkd->qbd', prob_rows, value_blocks, preferred_element_t...]
    all_to_all x3 -> x0, waiting for transfers between devices: 31.9 us -> none  [the longest x1 16.4 us: on_device(): lax.all_to_all(by_part(key_heads), 'seq', split_axis=1, concat_axis=0, ti...]
    all_to_all x1 -> x0, blocking collectives: 31.5 us -> none  [on_device(): lax.all_to_all(attended.reshape(seq_count * part_rows, 1, HD), 'seq', spl...]
    dot_general x4 -> x0, local copies, waits for them, and re-layouts: 17.6 us -> none  [the longest x2 9.61 us: on_device(): jnp.dot(normed, w_qkv[1], preferred_element_type=jnp.float32)]
    all_to_all x3 -> x0, starting transfers between devices: 16.2 us -> none  [the longest x1 8.23 us: on_device(): lax.all_to_all(by_part(key_heads), 'seq', split_axis=1, concat_axis=0, ti...]
  transfers between devices with their start and end apart: 8 -> 2, of which waited for: 5 -> 1; matrix products, arithmetic and copies ran while one was open for 27% -> 1% of each run, Pallas kernels for 0% -> 0%
where the time goes in v1:
time: 178 us; the launch traced here: 176 us
  Pallas kernels  162 us (91%)
  local copies, waits for them, and re-layouts  5.62 us (3%)
  starting transfers between devices  3.79 us (2%)
  waiting for transfers between devices  2.7 us (2%)
    pallas_call x1, Pallas kernels, exchange(): pl.pallas_call(functools.partial(exchange_kernel, seqs, segs, groups), in...  69.5 us
    pallas_call x1, Pallas kernels, finish(): pl.pallas_call(functools.partial(finish_kernel, seqs, groups, CHUNKS), in...  57.5 us
    pallas_call x1, Pallas kernels, attend(): pl.pallas_call(functools.partial(attend_kernel, blocks_source, blocks_par...  20.8 us
    pallas_call x1, Pallas kernels, front(): pl.pallas_call(functools.partial(front_kernel, heads), grid=(rows // tile...  13.9 us
    unnamed x16, local copies, waits for them, and re-layouts  5.31 us
  transfers between devices with their start and end apart: 2, of which 1 were waited for; matrix products, arithmetic and copies ran while one was open for 1% of the time, Pallas kernels for 0%

profile of v1, /device:TPU:0, one launch (start us, length us, event | category | flops | bytes accessed | tf_op | source)
XLA Modules:
  0.0 175.6 jit_solution(14944971867574339858)
XLA Ops:
  0.0 0.0 copy-start.4
  0.0 0.0 copy-start.5
  0.0 2.5 %collective-permute-start = (bf16[64,2048]{1,0:T(8,128)(2,1)}, bf16[64,2048]{1,0:T(8,128)(2,1)S(1)}, u32[]{:S(2)}, u32[]{:S(2)}) collective-permute-start(bf16[64,2048]{1,0:T(8,128)(2,1)} %param.10), channel_id=1, source_target_pairs={{0,1},{1,2},{2,3},{3,4},{4,5},{5,6},{6,7},{8,9},{9,10},{10,11},{11... | collective-permute-start | bytes 786440 | tf_op jit(solution)/shard_map/ppermute | solution.py:23
  2.5 1.3 collective-permute-start.1
  3.8 0.7 broadcast_subtract_fusion
  4.5 0.2 copy.11.place
  4.7 0.8 copy.10
  5.5 0.1 reshape.15.lists
  5.6 0.0 collective-permute-done
  5.6 2.7 %collective-permute-done.1 = bf16[64,2048]{1,0:T(8,128)(2,1)S(1)} collective-permute-done((bf16[64,2048]{1,0:T(8,128)(2,1)}, bf16[64,2048]{1,0:T(8,128)(2,1)S(1)}, u32[]{:S(2)}, u32[]{:S(2)}) %collective-permute-start.1) | collective-permute-done | bytes 262176 | tf_op jit(solution)/shard_map/ppermute | solution.py:24
  8.3 1.0 pad_maximum_fusion.base
  9.3 0.0 copy-done.4
  9.4 0.0 copy-done.5
  9.4 13.9 %front.1 = (bf16[4,1024,128]{2,1,0:T(8,128)(2,1)S(1)}, bf16[4,2,1024,128]{3,2,1,0:T(8,128)(2,1)S(1)}, f32[1024,512]{1,0:T(8,128)}) custom-call(bf16[1024,2048]{1,0:T(8,128)(2,1)} %sr.1, bf16[192,2048]{1,0:T(8,128)(2,1)S(1)} %pad_maximum_fusion.base, s32[1024,1]{1,0:T(8,128)S(1)} %copy.11.place, f32[1,2048]{1,0:T(1,128)S(1)} %bitcast.9, ...), custom_call_target="tpu_custom_call" | custom-call | tf_op jit(solution)/shard_map/front/pallas_call | solution.py:63
  23.3 0.0 copy-start.1
  23.3 1.3 copy-done.1
  24.6 0.0 copy-start.2
  24.7 1.0 copy-done.2
  25.6 0.0 copy-start.6
  25.6 69.5 %exchange.1 = (bf16[2,8192,128]{2,1,0:T(8,128)(2,1)}, bf16[8,512,128]{2,1,0:T(8,128)(2,1)}, bf16[2048,512]{1,0:T(8,128)(2,1)}) custom-call(bf16[4,1024,128]{2,1,0:T(8,128)(2,1)} %copy-done.2, bf16[4,2,1024,128]{3,2,1,0:T(8,128)(2,1)} %copy-done.1, bf16[512,2048]{1,0:T(8,128)(2,1)} %w_out.1), custom_call_target="tpu_custom_call" | custom-call | tf_op jit(solution)/shard_map/exchange/pallas_call | solution.py:221
  95.1 0.0 copy-done.6
  95.1 0.0 copy-start.3
  95.1 1.2 copy-done.3
  96.4 0.0 copy-start
  96.4 20.8 %attend.1 = bf16[4096,128]{1,0:T(8,128)(2,1)S(1)} custom-call(s32[1024]{0:T(1024)S(1)} %reshape.15.lists, s32[128]{0:T(128)S(1)} %copy-done.6, bf16[4096,128]{1,0:T(8,128)(2,1)S(1)} %bitcast.8, bf16[2,8192,128]{2,1,0:T(8,128)(2,1)} %get-tuple-element.14.kv), custom_call_target="tpu_custom_call" | custom-call | tf_op jit(solution)/shard_map/attend/pallas_call | solution.py:271
  117.1 0.0 copy-done
  117.1 57.5 %finish.1 = bf16[2,512,512]{2,1,0:T(8,128)(2,1)S(1)} custom-call(bf16[8,512,128]{2,1,0:T(8,128)(2,1)S(1)} %bitcast.7, bf16[2048,512]{1,0:T(8,128)(2,1)S(1)} %copy-done, f32[2,512,512]{2,1,0:T(8,128)} %bitcast.10), custom_call_target="tpu_custom_call" | custom-call | tf_op jit(solution)/shard_map/finish/pallas_call | solution.py:384
  174.7 1.0 copy.13
Async XLA Ops:
  0.0 9.4 %copy-start.4 = (f32[2048]{0:T(1024)S(1)}, f32[2048]{0:T(1024)}, u32[]{:S(2)}) copy-start(f32[2048]{0:T(1024)} %param.12) | copy-start | bytes 24580
  0.0 9.4 %copy-start.5 = (f32[2,512]{1,0:T(2,128)S(1)}, f32[2,512]{1,0:T(2,128)}, u32[]{:S(2)}) copy-start(f32[2,512]{1,0:T(2,128)} %qk_gain.1) | copy-start | bytes 12292
  0.0 5.6 %collective-permute-start = (bf16[64,2048]{1,0:T(8,128)(2,1)}, bf16[64,2048]{1,0:T(8,128)(2,1)S(1)}, u32[]{:S(2)}, u32[]{:S(2)}) collective-permute-start(bf16[64,2048]{1,0:T(8,128)(2,1)} %param.10), channel_id=1, source_target_pairs={{0,1},{1,2},{2,3},{3,4},{4,5},{5,6},{6,7},{8,9},{9,10},{10,11},{11... | collective-permute-start | bytes 786440 | tf_op jit(solution)/shard_map/ppermute | solution.py:23
  2.5 5.8 %collective-permute-start.1 = (bf16[64,2048]{1,0:T(8,128)(2,1)}, bf16[64,2048]{1,0:T(8,128)(2,1)S(1)}, u32[]{:S(2)}, u32[]{:S(2)}) collective-permute-start(bf16[64,2048]{1,0:T(8,128)(2,1)} %param.10), channel_id=1, source_target_pairs={{1,0},{2,1},{3,2},{4,3},{5,4},{6,5},{7,6},{9,8},{10,9},{11,10},{12... | collective-permute-start | bytes 786440 | tf_op jit(solution)/shard_map/ppermute | solution.py:24
  23.3 1.3 copy-start.1
  24.6 1.0 copy-start.2
  25.6 69.5 %copy-start.6 = (s32[128]{0:T(128)S(1)}, s32[128]{0:T(128)}, u32[]{:S(2)}) copy-start(s32[128]{0:T(128)} %counts.1) | copy-start | bytes 1540
  95.1 1.2 copy-start.3
  96.4 20.8 %copy-start = (bf16[2048,512]{1,0:T(8,128)(2,1)S(1)}, bf16[2048,512]{1,0:T(8,128)(2,1)}, u32[]{:S(2)}) copy-start(bf16[2048,512]{1,0:T(8,128)(2,1)} %get-tuple-element.15.w_cols) | copy-start | bytes 6291460

commit v2 on v1

v2 whole, which is shorter than its diff:
```python
import functools

import jax
import jax.numpy as jnp
from jax import lax
from jax.experimental import pallas as pl
from jax.experimental.pallas import tpu as pltpu
from jax.sharding import PartitionSpec as P

HD = 128
BASE_FT = 64
BLOCK = 64
EPSILON = 1e-06
CHUNKS = 4
TOGETHER = 4
MESH = pl.DeviceIdType.MESH
MIB = 2**20


def padded_2(x, axis, width):
    count, length = lax.axis_size(axis), x.shape[0]
    up = [(i, (i + 1) % count) for i in range(count - 1)]
    down = [(j, i) for i, j in up]
    before = lax.ppermute(lax.slice_in_dim(x, length - width, length, axis=0), axis, up)
    after = lax.ppermute(lax.slice_in_dim(x, 0, width, axis=0), axis, down)
    return jnp.concatenate([before, x, after], axis=0)


def rms_scale(tensor):
    return lax.rsqrt(jnp.mean(tensor * tensor, axis=-1, keepdims=True) + EPSILON)


def front_kernel(heads, sr, base, place, gain, w_qkv, qk_gain, q_out, kv_out, share_out, mixed):
    rows = sr.shape[0]
    count = base.shape[0]
    hot = (lax.broadcasted_iota(jnp.int32, (rows, count), 1) == place[...]).astype(jnp.bfloat16)
    condition = jnp.dot(hot, base[...], preferred_element_type=jnp.float32)
    mixed[...] = sr[...].astype(jnp.float32) + condition
    width = share_out.shape[1]
    start = pl.multiple_of(lax.axis_index("segment") * width, width)
    share_out[...] = mixed[:, pl.ds(start, width)]
    whole = mixed[...]
    normed = (whole * rms_scale(whole) * gain[...]).astype(jnp.bfloat16)
    for which in range(3):
        raw = jnp.dot(normed, w_qkv[which], preferred_element_type=jnp.float32)
        for head in range(heads):
            cols = slice(head * HD, (head + 1) * HD)
            part = raw[:, cols]
            if which < 2:
                part = part * rms_scale(part) * qk_gain[which : which + 1, cols]
            part = part.astype(jnp.bfloat16)
            if which == 0:
                q_out[head] = part
            else:
                kv_out[head, which - 1] = part


def front(sr, base, place, gain, w_qkv, qk_gain):
    rows, depth = sr.shape
    width = w_qkv.shape[2]
    heads = width // HD
    tile = 256
    share = depth // lax.axis_size("segment")
    return pl.pallas_call(
        functools.partial(front_kernel, heads),
        grid=(rows // tile,),
        in_specs=[
            pl.BlockSpec((tile, depth), lambda i: (i, 0)),
            pl.BlockSpec(base.shape, lambda i: (0, 0)),
            pl.BlockSpec((tile, 1), lambda i: (i, 0)),
            pl.BlockSpec((1, depth), lambda i: (0, 0)),
            pl.BlockSpec(w_qkv.shape, lambda i: (0, 0, 0)),
            pl.BlockSpec(qk_gain.shape, lambda i: (0, 0)),
        ],
        out_specs=[
            pl.BlockSpec((heads, tile, HD), lambda i: (0, i, 0)),
            pl.BlockSpec((heads, 2, tile, HD), lambda i: (0, 0, i, 0)),
            pl.BlockSpec((tile, share), lambda i: (i, 0)),
        ],
        out_shape=[
            jax.ShapeDtypeStruct((heads, rows, HD), jnp.bfloat16),
            jax.ShapeDtypeStruct((heads, 2, rows, HD), jnp.bfloat16),
            jax.ShapeDtypeStruct((rows, share), jnp.float32),
        ],
        scratch_shapes=[pltpu.VMEM((tile, depth), jnp.float32)],
        compiler_params=pltpu.CompilerParams(vmem_limit_bytes=48 * MIB),
        name="front",
    )(sr, base, place, gain, w_qkv, qk_gain)


def greet(targets):
    barrier = pltpu.get_barrier_semaphore()
    for target in targets:
        pl.semaphore_signal(barrier, inc=1, device_id=target, device_id_type=MESH)
    pl.semaphore_wait(barrier, len(targets))


def remote(src, dst, send, recv, target):
    return pltpu.make_async_remote_copy(
        src_ref=src, dst_ref=dst, send_sem=send, recv_sem=recv, device_id=target, device_id_type=MESH
    )


def middle_kernel(
    seqs, segs, groups, chunks, together,
    lists, counts, q, kv, w_out, share, out,
    kv_all, q_all, att, full, w_cols,
    kv_send, kv_recv, q_send, q_recv, fw_send, fw_recv, w_send, w_recv,
    z_send, z_recv, p_send, p_recv, own, own_chunk,
):
    me, seg = lax.axis_index("seq"), lax.axis_index("segment")
    rows = q.shape[1]
    part_rows = rows // groups
    size = part_rows // chunks
    half = size // 2
    head, part = me // groups, me % groups
    depth, cols = w_out.shape[0], w_out.shape[1] // segs
    window = lists.shape[0] // counts.shape[0]
    near_x, near_y, far = seg ^ 1, seg ^ 2, seg ^ 3
    greet([(seg, me ^ k) for k in range(1, seqs)] + [(seg ^ k, me) for k in range(1, segs)])

    blocks_source, blocks_part, blocks_chunk = rows // BLOCK, part_rows // BLOCK, size // BLOCK

    def blocks_of(which):
        return pl.ds(which * blocks_part, blocks_part)

    def chunk_rows(chunk):
        return pl.ds(pl.multiple_of(chunk * size, size), size)

    def landing(source, which):
        start = source * blocks_source + which * blocks_part
        return kv_all.at[:, pl.ds(start, blocks_part)]

    def kv_copy(target, source):
        return remote(
            kv.at[target // groups, :, blocks_of(target % groups)],
            landing(source, target % groups),
            kv_send.at[target],
            kv_recv.at[source],
            (seg, target),
        )

    def q_from(chunk, target):
        start = pl.multiple_of((target % groups) * part_rows + chunk * size, size)
        return q.at[target // groups, pl.ds(start, size), :]

    def q_copy(chunk, target, source):
        return remote(
            q_from(chunk, target),
            q_all.at[source, chunk_rows(chunk), :],
            q_send.at[chunk, target],
            q_recv.at[chunk, source],
            (seg, target),
        )

    def w_from(target):
        return w_out.at[:, pl.ds(pl.multiple_of(target * cols, cols), cols)]

    def w_to(source):
        return w_cols.at[pl.ds(pl.multiple_of(source * depth, depth), depth), :]

    def w_copy(target, source):
        return remote(
            w_from(target), w_to(source), w_send.at[target], w_recv.at[source], (target, me)
        )

    def forward(source, step, sender_part):
        slot = landing(source, sender_part)
        target = head * groups + lax.rem(part + step, groups)
        return remote(
            slot, slot, fw_send.at[source, step - 1], fw_recv.at[source, step - 1], (seg, target)
        )

    def spot(chunk, owner):
        lanes = pl.ds(pl.multiple_of((owner // groups) * HD, HD), HD)
        return full.at[seg, owner % groups, chunk_rows(chunk), lanes]

    def z_copy(chunk, target, owner):
        return remote(
            att.at[target, chunk_rows(chunk), :],
            spot(chunk, owner),
            z_send.at[chunk, target],
            z_recv.at[chunk, owner],
            (seg, target),
        )

    def own_copy(chunk):
        return pltpu.make_async_copy(
            att.at[me, chunk_rows(chunk), :], spot(chunk, me), own_chunk.at[chunk]
        )

    def pair_copy(chunk, kind, origin, to):
        at = pl.multiple_of(chunk * size + (half if kind == 3 else 0), half)
        piece = full.at[origin, :, pl.ds(at, size if kind < 2 else half), :]
        return remote(piece, piece, p_send.at[chunk, kind], p_recv.at[chunk, kind], (to, me))

    own_kv = pltpu.make_async_copy(kv.at[head, :, blocks_of(part)], landing(me, part), own.at[0])
    own_q = pltpu.make_async_copy(
        q.at[head, pl.ds(pl.multiple_of(part * part_rows, part_rows), part_rows), :], q_all.at[me], own.at[1]
    )
    own_w = pltpu.make_async_copy(w_from(seg), w_to(seg), own.at[2])
    own_kv.start()

    @pl.loop(1, seqs)
    def _(k):
        kv_copy(me ^ (seqs - k), me).start()

    own_q.start()
    own_w.start()

    @pl.loop(1, segs)
    def _(k):
        w_copy(seg ^ k, seg).start()

    own_kv.wait()
    for step in range(1, groups):
        forward(me, step, part).start()

    @pl.loop(1, seqs)
    def _(k):
        other = me ^ k
        kv_copy(me, other).wait_recv()
        for step in range(1, groups):
            forward(other, step, part).start()
        kv_copy(other, me).wait_send()

        @pl.loop(0, chunks)
        def _(chunk):
            q_copy(chunk, other, me).start()

    @pl.loop(0, seqs)
    def _(source):
        for step in range(1, groups):
            forward(source, step, lax.rem(part + groups - step, groups)).wait_recv()
            forward(source, step, part).wait_send()

    own_q.wait()

    column = lax.broadcasted_iota(jnp.int32, (BLOCK, window * BLOCK), 1)

    def one(source, local):
        block = source * blocks_source + part * blocks_part + local
        listed = [lists[block * window + w] for w in range(window)]
        keys = jnp.concatenate([kv_all[0, at] for at in listed], axis=0)
        values = jnp.concatenate([kv_all[1, at] for at in listed], axis=0)
        query = q_all[source, pl.ds(pl.multiple_of(local * BLOCK, BLOCK), BLOCK), :]
        scores = lax.dot_general(
            query, keys, (((1,), (1,)), ((), ())), preferred_element_type=jnp.float32
        ) * HD ** (-0.5)
        scores = jnp.where(column < counts[block] * BLOCK, scores, -jnp.inf)
        weights = jnp.exp(scores - jnp.max(scores, axis=1, keepdims=True))
        total = jnp.sum(weights, axis=1, keepdims=True)
        summed = jnp.dot(weights.astype(jnp.bfloat16), values, preferred_element_type=jnp.float32)
        return (summed / total).astype(jnp.bfloat16)

    def attend(chunk):
        @pl.loop(0, seqs * blocks_chunk // together)
        def _(step):
            places = []
            for i in range(together):
                index = step * together + i
                places.append((index // blocks_chunk, chunk * blocks_chunk + index % blocks_chunk))
            done = [one(*place) for place in places]
            for (source, local), value in zip(places, done):
                att[source, pl.ds(pl.multiple_of(local * BLOCK, BLOCK), BLOCK), :] = value

    @pl.loop(0, chunks + 3)
    def _(step):
        @pl.when(step < chunks)
        def _():
            @pl.loop(1, seqs)
            def _(k):
                q_copy(step, me, me ^ k).wait_recv()

            attend(step)

            @pl.loop(1, seqs)
            def _(k):
                z_copy(step, me ^ (seqs - k), me).start()

            own_copy(step).start()

        @pl.when(jnp.logical_and(step >= 1, step < chunks + 1))
        def _():
            chunk = step - 1
            own_copy(chunk).wait()

            @pl.loop(1, seqs)
            def _(k):
                z_copy(chunk, me, me ^ k).wait_recv()

            pair_copy(chunk, 0, seg, near_x).start()
            pair_copy(chunk, 1, seg, near_y).start()

        @pl.when(jnp.logical_and(step >= 2, step < chunks + 2))
        def _():
            chunk = step - 2
            pair_copy(chunk, 0, near_x, near_x).wait_recv()
            pair_copy(chunk, 2, near_x, near_y).start()
            pair_copy(chunk, 1, near_y, near_y).wait_recv()
            pair_copy(chunk, 3, near_y, near_x).start()

        @pl.when(step == 3)
        def _():
            own_w.wait()

            @pl.loop(1, segs)
            def _(k):
                w_copy(seg, seg ^ k).wait_recv()

        @pl.when(step >= 3)
        def _():
            chunk = step - 3
            pair_copy(chunk, 2, far, near_y).wait_recv()
            pair_copy(chunk, 3, far, near_x).wait_recv()
            here = chunk_rows(chunk)
            total = jnp.zeros((groups * size, cols), jnp.float32)
            for j in range(segs):
                piece = full[j, :, here, :].reshape(groups * size, depth)
                total += jnp.dot(
                    piece, w_cols[j * depth : (j + 1) * depth, :], preferred_element_type=jnp.float32
                )
            total = total.reshape(groups, size, cols)
            out[:, here, :] = (share[:, here, :] + total).astype(jnp.bfloat16)

    @pl.loop(0, chunks)
    def _(chunk):
        pair_copy(chunk, 0, seg, near_x).wait_send()
        pair_copy(chunk, 1, seg, near_y).wait_send()
        pair_copy(chunk, 2, near_x, near_y).wait_send()
        pair_copy(chunk, 3, near_y, near_x).wait_send()

        @pl.loop(1, seqs)
        def _(k):
            q_copy(chunk, me ^ k, me).wait_send()
            z_copy(chunk, me ^ k, me).wait_send()

    @pl.loop(1, segs)
    def _(k):
        w_copy(seg ^ k, seg).wait_send()


def middle(lists, counts, q, kv, w_out, share, seqs, segs, groups):
    heads, rows, _ = q.shape
    depth, width = w_out.shape
    part_rows = rows // groups
    chunks = min(CHUNKS, part_rows // BLOCK)
    cols = width // segs
    dma = pltpu.SemaphoreType.DMA
    anywhere = pl.BlockSpec(memory_space=pl.ANY)
    vmem = pl.BlockSpec(memory_space=pltpu.VMEM)
    smem = pl.BlockSpec(memory_space=pltpu.SMEM)
    return pl.pallas_call(
        functools.partial(middle_kernel, seqs, segs, groups, chunks, TOGETHER),
        in_specs=[smem, smem, anywhere, anywhere, anywhere, vmem],
        out_specs=vmem,
        out_shape=jax.ShapeDtypeStruct((groups, part_rows, cols), jnp.bfloat16),
        scratch_shapes=[
            pltpu.VMEM((2, seqs * rows // BLOCK, BLOCK, HD), jnp.bfloat16),
            pltpu.VMEM((seqs, part_rows, HD), jnp.bfloat16),
            pltpu.VMEM((seqs, part_rows, HD), jnp.bfloat16),
            pltpu.VMEM((segs, groups, part_rows, depth), jnp.bfloat16),
            pltpu.VMEM((segs * depth, cols), jnp.bfloat16),
            dma((seqs,)), dma((seqs,)), dma((chunks, seqs)), dma((chunks, seqs)),
            dma((seqs, max(groups - 1, 1))), dma((seqs, max(groups - 1, 1))),
            dma((segs,)), dma((segs,)),
            dma((chunks, seqs)), dma((chunks, seqs)), dma((chunks, 4)), dma((chunks, 4)),
            dma((3,)), dma((chunks,)),
        ],
        compiler_params=pltpu.CompilerParams(
            collective_id=0, has_side_effects=True, vmem_limit_bytes=48 * MIB
        ),
        name="middle",
    )(lists, counts, q, kv.reshape(heads, 2, rows // BLOCK, BLOCK, HD), w_out, share)


def on_device(
    sr_tokens, base_latent, upsample_map, norm_gain, w_qkv, qk_gain, w_out, block_lists, block_counts
):
    seqs, segs = lax.axis_size("seq"), lax.axis_size("segment")
    rank = lax.axis_index("seq")
    rows = sr_tokens.shape[0]
    heads = w_qkv.shape[2] // HD
    groups = seqs // heads
    part_rows = rows // groups
    padded = padded_2(base_latent, "seq", BASE_FT)
    place = (upsample_map - (rank * base_latent.shape[0] - BASE_FT))[:, None]
    q, kv, share = front(sr_tokens, padded, place, norm_gain[None], w_qkv, qk_gain)
    out = middle(
        block_lists.reshape(-1), block_counts, q, kv, w_out,
        share.reshape(groups, part_rows, -1), seqs, segs, groups,
    )
    return out.reshape(rows, -1)


def solution(mesh):
    placed = (
        P("seq", None),
        P("seq", None),
        P("seq"),
        P(),
        P(None, None, "segment"),
        P(None, "segment"),
        P("segment", None),
        P(),
        P(),
    )
    return jax.shard_map(
        on_device, mesh=mesh, in_specs=placed, out_specs=P("seq", "segment"), check_vma=False
    )
```

time: 178 us -> 152 us (0.85); the launches traced: 176 us -> 151 us
  Pallas kernels: 162 us -> 141 us
  local copies, waits for them, and re-layouts: 5.62 us -> 2.09 us
    pallas_call x3 -> x1, Pallas kernels: 148 us -> 127 us  [middle(): pl.pallas_call(functools.partial(middle_kernel, seqs, segs, groups, chunk...]
    unnamed x16 -> x8, local copies, waits for them, and re-layouts: 5.31 us -> 1.78 us
where the time goes in v2:
time: 152 us; the launch traced here: 151 us
  Pallas kernels  141 us (93%)
  starting transfers between devices  3.79 us (2%)
  waiting for transfers between devices  2.7 us (2%)
  local copies, waits for them, and re-layouts  2.09 us (1%)
  other arithmetic  1.71 us (1%)
    pallas_call x1, Pallas kernels, middle(): pl.pallas_call(functools.partial(middle_kernel, seqs, segs, groups, chunk...  127 us
    pallas_call x1, Pallas kernels, front(): pl.pallas_call(functools.partial(front_kernel, heads), grid=(rows // tile...  13.9 us
  transfers between devices with their start and end apart: 2, of which 1 were waited for; matrix products, arithmetic and copies ran while one was open for 1% of the time, Pallas kernels for 0%

profile of v2, /device:TPU:0, one launch (start us, length us, event | category | flops | bytes accessed | tf_op | source)
XLA Modules:
  0.0 151.5 jit_solution(10019233772751989684)
XLA Ops:
  0.0 0.0 copy-start
  0.0 0.0 copy-start.1
  0.0 2.5 %collective-permute-start = (bf16[64,2048]{1,0:T(8,128)(2,1)}, bf16[64,2048]{1,0:T(8,128)(2,1)S(1)}, u32[]{:S(2)}, u32[]{:S(2)}) collective-permute-start(bf16[64,2048]{1,0:T(8,128)(2,1)} %param.10), channel_id=1, source_target_pairs={{0,1},{1,2},{2,3},{3,4},{4,5},{5,6},{6,7},{8,9},{9,10},{10,11},{11... | collective-permute-start | bytes 786440 | tf_op jit(solution)/shard_map/ppermute | solution.py:24
  2.5 1.3 collective-permute-start.1
  3.8 0.7 broadcast_subtract_fusion
  4.5 0.2 copy.11.place
  4.7 0.8 copy.10
  5.5 0.1 reshape.12.lists
  5.6 0.0 collective-permute-done
  5.6 2.7 %collective-permute-done.1 = bf16[64,2048]{1,0:T(8,128)(2,1)S(1)} collective-permute-done((bf16[64,2048]{1,0:T(8,128)(2,1)}, bf16[64,2048]{1,0:T(8,128)(2,1)S(1)}, u32[]{:S(2)}, u32[]{:S(2)}) %collective-permute-start.1) | collective-permute-done | bytes 262176 | tf_op jit(solution)/shard_map/ppermute | solution.py:25
  8.3 1.0 pad_maximum_fusion.base
  9.3 0.0 copy-done
  9.4 0.0 copy-done.1
  9.4 0.0 copy-start.2
  9.4 13.9 %front.1 = (bf16[4,1024,128]{2,1,0:T(8,128)(2,1)S(1)}, bf16[4,2,1024,128]{3,2,1,0:T(8,128)(2,1)S(1)}, f32[1024,512]{1,0:T(8,128)}) custom-call(bf16[1024,2048]{1,0:T(8,128)(2,1)} %sr.1, bf16[192,2048]{1,0:T(8,128)(2,1)S(1)} %pad_maximum_fusion.base, s32[1024,1]{1,0:T(8,128)S(1)} %copy.11.place, f32[1,2048]{1,0:T(1,128)S(1)} %bitcast.7, ...), custom_call_target="tpu_custom_call" | custom-call | tf_op jit(solution)/shard_map/front/pallas_call | solution.py:64
  23.3 0.0 copy-done.2
  23.3 127.2 %middle.1 = bf16[2,512,512]{2,1,0:T(8,128)(2,1)S(1)} custom-call(s32[1024]{0:T(1024)S(1)} %reshape.12.lists, s32[128]{0:T(128)S(1)} %copy-done.2, bf16[4,1024,128]{2,1,0:T(8,128)(2,1)S(1)} %get-tuple-element.8.q, bf16[4,2,16,64,128]{4,3,2,1,0:T(8,128)(2,1)S(1)} %bitcast.6, bf16[512,2048]{1,0:T(8,128)(2,1)} %w_out.1, f32[2,512,512]{2,1,0:T(8,128)} %bitcast.8), custom_call_target="tpu_custom_call" | custom-call | tf_op jit(solution)/shard_map/middle/pallas_call | solution.py:353
  150.5 1.0 copy.13
Async XLA Ops:
  0.0 9.4 %copy-start = (f32[2048]{0:T(1024)S(1)}, f32[2048]{0:T(1024)}, u32[]{:S(2)}) copy-start(f32[2048]{0:T(1024)} %param.12) | copy-start | bytes 24580
  0.0 9.4 %copy-start.1 = (f32[2,512]{1,0:T(2,128)S(1)}, f32[2,512]{1,0:T(2,128)}, u32[]{:S(2)}) copy-start(f32[2,512]{1,0:T(2,128)} %qk_gain.1) | copy-start | bytes 12292
  0.0 5.6 %collective-permute-start = (bf16[64,2048]{1,0:T(8,128)(2,1)}, bf16[64,2048]{1,0:T(8,128)(2,1)S(1)}, u32[]{:S(2)}, u32[]{:S(2)}) collective-permute-start(bf16[64,2048]{1,0:T(8,128)(2,1)} %param.10), channel_id=1, source_target_pairs={{0,1},{1,2},{2,3},{3,4},{4,5},{5,6},{6,7},{8,9},{9,10},{10,11},{11... | collective-permute-start | bytes 786440 | tf_op jit(solution)/shard_map/ppermute | solution.py:24
  2.5 5.8 %collective-permute-start.1 = (bf16[64,2048]{1,0:T(8,128)(2,1)}, bf16[64,2048]{1,0:T(8,128)(2,1)S(1)}, u32[]{:S(2)}, u32[]{:S(2)}) collective-permute-start(bf16[64,2048]{1,0:T(8,128)(2,1)} %param.10), channel_id=1, source_target_pairs={{1,0},{2,1},{3,2},{4,3},{5,4},{6,5},{7,6},{9,8},{10,9},{11,10},{12... | collective-permute-start | bytes 786440 | tf_op jit(solution)/shard_map/ppermute | solution.py:25
  9.4 14.0 %copy-start.2 = (s32[128]{0:T(128)S(1)}, s32[128]{0:T(128)}, u32[]{:S(2)}) copy-start(s32[128]{0:T(128)} %counts.1) | copy-start | bytes 1540

commit v3 on v2

--- a/solution.py
+++ b/solution.py
@@ -11,7 +11,7 @@
 BASE_FT = 64
 BLOCK = 64
 EPSILON = 1e-06
-CHUNKS = 4
+CHUNKS = 8
 TOGETHER = 4
 MESH = pl.DeviceIdType.MESH
 MIB = 2**20

time: 152 us -> 152 us (level)
  no operation moved by 1% of the time
where the time goes in v3:
time: 152 us; the launch traced here: 151 us
  Pallas kernels  141 us (93%)
  starting transfers between devices  3.79 us (2%)
  waiting for transfers between devices  2.7 us (2%)
  local copies, waits for them, and re-layouts  2.09 us (1%)
  other arithmetic  1.71 us (1%)
    pallas_call x1, Pallas kernels, middle(): pl.pallas_call(functools.partial(middle_kernel, seqs, segs, groups, chunk...  127 us
    pallas_call x1, Pallas kernels, front(): pl.pallas_call(functools.partial(front_kernel, heads), grid=(rows // tile...  13.9 us
  transfers between devices with their start and end apart: 2, of which 1 were waited for; matrix products, arithmetic and copies ran while one was open for 1% of the time, Pallas kernels for 0%

profile of v3, /device:TPU:0, one launch (start us, length us, event | category | flops | bytes accessed | tf_op | source)
XLA Modules:
  0.0 151.4 jit_solution(18280815833380640502)
XLA Ops:
  0.0 0.0 copy-start
  0.0 0.0 copy-start.1
  0.0 2.5 %collective-permute-start = (bf16[64,2048]{1,0:T(8,128)(2,1)}, bf16[64,2048]{1,0:T(8,128)(2,1)S(1)}, u32[]{:S(2)}, u32[]{:S(2)}) collective-permute-start(bf16[64,2048]{1,0:T(8,128)(2,1)} %param.10), channel_id=1, source_target_pairs={{0,1},{1,2},{2,3},{3,4},{4,5},{5,6},{6,7},{8,9},{9,10},{10,11},{11... | collective-permute-start | bytes 786440 | tf_op jit(solution)/shard_map/ppermute | solution.py:24
  2.5 1.3 collective-permute-start.1
  3.8 0.7 broadcast_subtract_fusion
  4.5 0.2 copy.11.place
  4.7 0.8 copy.10
  5.5 0.1 reshape.12.lists
  5.6 0.0 collective-permute-done
  5.6 2.7 %collective-permute-done.1 = bf16[64,2048]{1,0:T(8,128)(2,1)S(1)} collective-permute-done((bf16[64,2048]{1,0:T(8,128)(2,1)}, bf16[64,2048]{1,0:T(8,128)(2,1)S(1)}, u32[]{:S(2)}, u32[]{:S(2)}) %collective-permute-start.1) | collective-permute-done | bytes 262176 | tf_op jit(solution)/shard_map/ppermute | solution.py:25
  8.3 1.0 pad_maximum_fusion.base
  9.3 0.0 copy-done
  9.4 0.0 copy-done.1
  9.4 0.0 copy-start.2
  9.4 13.9 %front.1 = (bf16[4,1024,128]{2,1,0:T(8,128)(2,1)S(1)}, bf16[4,2,1024,128]{3,2,1,0:T(8,128)(2,1)S(1)}, f32[1024,512]{1,0:T(8,128)}) custom-call(bf16[1024,2048]{1,0:T(8,128)(2,1)} %sr.1, bf16[192,2048]{1,0:T(8,128)(2,1)S(1)} %pad_maximum_fusion.base, s32[1024,1]{1,0:T(8,128)S(1)} %copy.11.place, f32[1,2048]{1,0:T(1,128)S(1)} %bitcast.7, ...), custom_call_target="tpu_custom_call" | custom-call | tf_op jit(solution)/shard_map/front/pallas_call | solution.py:64
  23.3 0.0 copy-done.2
  23.3 127.0 %middle.1 = bf16[2,512,512]{2,1,0:T(8,128)(2,1)S(1)} custom-call(s32[1024]{0:T(1024)S(1)} %reshape.12.lists, s32[128]{0:T(128)S(1)} %copy-done.2, bf16[4,1024,128]{2,1,0:T(8,128)(2,1)S(1)} %get-tuple-element.8.q, bf16[4,2,16,64,128]{4,3,2,1,0:T(8,128)(2,1)S(1)} %bitcast.6, bf16[512,2048]{1,0:T(8,128)(2,1)} %w_out.1, f32[2,512,512]{2,1,0:T(8,128)} %bitcast.8), custom_call_target="tpu_custom_call" | custom-call | tf_op jit(solution)/shard_map/middle/pallas_call | solution.py:353
  150.4 1.0 copy.13
Async XLA Ops:
  0.0 9.4 %copy-start = (f32[2048]{0:T(1024)S(1)}, f32[2048]{0:T(1024)}, u32[]{:S(2)}) copy-start(f32[2048]{0:T(1024)} %param.12) | copy-start | bytes 24580
  0.0 9.4 %copy-start.1 = (f32[2,512]{1,0:T(2,128)S(1)}, f32[2,512]{1,0:T(2,128)}, u32[]{:S(2)}) copy-start(f32[2,512]{1,0:T(2,128)} %qk_gain.1) | copy-start | bytes 12292
  0.0 5.6 %collective-permute-start = (bf16[64,2048]{1,0:T(8,128)(2,1)}, bf16[64,2048]{1,0:T(8,128)(2,1)S(1)}, u32[]{:S(2)}, u32[]{:S(2)}) collective-permute-start(bf16[64,2048]{1,0:T(8,128)(2,1)} %param.10), channel_id=1, source_target_pairs={{0,1},{1,2},{2,3},{3,4},{4,5},{5,6},{6,7},{8,9},{9,10},{10,11},{11... | collective-permute-start | bytes 786440 | tf_op jit(solution)/shard_map/ppermute | solution.py:24
  2.5 5.8 %collective-permute-start.1 = (bf16[64,2048]{1,0:T(8,128)(2,1)}, bf16[64,2048]{1,0:T(8,128)(2,1)S(1)}, u32[]{:S(2)}, u32[]{:S(2)}) collective-permute-start(bf16[64,2048]{1,0:T(8,128)(2,1)} %param.10), channel_id=1, source_target_pairs={{1,0},{2,1},{3,2},{4,3},{5,4},{6,5},{7,6},{9,8},{10,9},{11,10},{12... | collective-permute-start | bytes 786440 | tf_op jit(solution)/shard_map/ppermute | solution.py:25
  9.4 14.0 %copy-start.2 = (s32[128]{0:T(128)S(1)}, s32[128]{0:T(128)}, u32[]{:S(2)}) copy-start(s32[128]{0:T(128)} %counts.1) | copy-start | bytes 1540

commit v4 on v3

--- a/solution.py
+++ b/solution.py
@@ -30,7 +30,7 @@
     return lax.rsqrt(jnp.mean(tensor * tensor, axis=-1, keepdims=True) + EPSILON)
 
 
-def front_kernel(heads, sr, base, place, gain, w_qkv, qk_gain, q_out, kv_out, share_out, mixed):
+def front_kernel(heads, sr, base, place, gain, w_qkv, qk_gain, normed_out, kv_out, share_out, mixed):
     rows = sr.shape[0]
     count = base.shape[0]
     hot = (lax.broadcasted_iota(jnp.int32, (rows, count), 1) == place[...]).astype(jnp.bfloat16)
@@ -41,18 +41,15 @@
     share_out[...] = mixed[:, pl.ds(start, width)]
     whole = mixed[...]
     normed = (whole * rms_scale(whole) * gain[...]).astype(jnp.bfloat16)
-    for which in range(3):
+    normed_out[...] = normed
+    for which in range(2):
         raw = jnp.dot(normed, w_qkv[which], preferred_element_type=jnp.float32)
         for head in range(heads):
             cols = slice(head * HD, (head + 1) * HD)
             part = raw[:, cols]
-            if which < 2:
-                part = part * rms_scale(part) * qk_gain[which : which + 1, cols]
-            part = part.astype(jnp.bfloat16)
             if which == 0:
-                q_out[head] = part
-            else:
-                kv_out[head, which - 1] = part
+                part = part * rms_scale(part) * qk_gain[1:2, cols]
+            kv_out[head, which] = part.astype(jnp.bfloat16)
 
 
 def front(sr, base, place, gain, w_qkv, qk_gain):
@@ -69,16 +66,16 @@
             pl.BlockSpec(base.shape, lambda i: (0, 0)),
             pl.BlockSpec((tile, 1), lambda i: (i, 0)),
             pl.BlockSpec((1, depth), lambda i: (0, 0)),
-            pl.BlockSpec(w_qkv.shape, lambda i: (0, 0, 0)),
+            pl.BlockSpec((pl.Element(2), pl.Element(depth), pl.Element(width)), lambda i: (1, 0, 0)),
             pl.BlockSpec(qk_gain.shape, lambda i: (0, 0)),
         ],
         out_specs=[
-            pl.BlockSpec((heads, tile, HD), lambda i: (0, i, 0)),
+            pl.BlockSpec((tile, depth), lambda i: (i, 0)),
             pl.BlockSpec((heads, 2, tile, HD), lambda i: (0, 0, i, 0)),
             pl.BlockSpec((tile, share), lambda i: (i, 0)),
         ],
         out_shape=[
-            jax.ShapeDtypeStruct((heads, rows, HD), jnp.bfloat16),
+            jax.ShapeDtypeStruct((rows, depth), jnp.bfloat16),
             jax.ShapeDtypeStruct((heads, 2, rows, HD), jnp.bfloat16),
             jax.ShapeDtypeStruct((rows, share), jnp.float32),
         ],
@@ -103,13 +100,17 @@
 
 def middle_kernel(
     seqs, segs, groups, chunks, together,
-    lists, counts, q, kv, w_out, share, out,
-    kv_all, q_all, att, full, w_cols,
+    lists, counts, normed, w_qkv, qk_gain, kv, w_out, share, out,
+    q, rows_in, w_q, kv_all, q_all, att, full, w_cols,
     kv_send, kv_recv, q_send, q_recv, fw_send, fw_recv, w_send, w_recv,
     z_send, z_recv, p_send, p_recv, own, own_chunk,
 ):
     me, seg = lax.axis_index("seq"), lax.axis_index("segment")
     rows = q.shape[1]
+    load_rows = pltpu.make_async_copy(normed, rows_in, own.at[3])
+    load_w = pltpu.make_async_copy(w_qkv.at[0], w_q, own.at[4])
+    load_rows.start()
+    load_w.start()
     part_rows = rows // groups
     size = part_rows // chunks
     half = size // 2
@@ -205,7 +206,6 @@
     def _(k):
         kv_copy(me ^ (seqs - k), me).start()
 
-    own_q.start()
     own_w.start()
 
     @pl.loop(1, segs)
@@ -215,6 +215,22 @@
     own_kv.wait()
     for step in range(1, groups):
         forward(me, step, part).start()
+
+    load_rows.wait()
+    load_w.wait()
+    tile = 256
+
+    @pl.loop(0, rows // tile)
+    def _(i):
+        here = pl.ds(pl.multiple_of(i * tile, tile), tile)
+        raw = jnp.dot(rows_in[here, :], w_q[...], preferred_element_type=jnp.float32)
+        for h in range(q.shape[0]):
+            lanes = slice(h * HD, (h + 1) * HD)
+            piece = raw[:, lanes]
+            piece = piece * rms_scale(piece) * qk_gain[0:1, lanes]
+            q[h, here, :] = piece.astype(jnp.bfloat16)
+
+    own_q.start()
 
     @pl.loop(1, seqs)
     def _(k):
@@ -223,10 +239,13 @@
         for step in range(1, groups):
             forward(other, step, part).start()
         kv_copy(other, me).wait_send()
-
-        @pl.loop(0, chunks)
-        def _(chunk):
-            q_copy(chunk, other, me).start()
+        q_copy(0, other, me).start()
+
+    @pl.loop(1, chunks)
+    def _(chunk):
+        @pl.loop(1, seqs)
+        def _(k):
+            q_copy(chunk, me ^ (seqs - k), me).start()
 
     @pl.loop(0, seqs)
     def _(source):
@@ -340,8 +359,8 @@
         w_copy(seg ^ k, seg).wait_send()
 
 
-def middle(lists, counts, q, kv, w_out, share, seqs, segs, groups):
-    heads, rows, _ = q.shape
+def middle(lists, counts, normed, w_qkv, qk_gain, kv, w_out, share, seqs, segs, groups):
+    heads, _, rows, _ = kv.shape
     depth, width = w_out.shape
     part_rows = rows // groups
     chunks = min(CHUNKS, part_rows // BLOCK)
@@ -352,10 +371,13 @@
     smem = pl.BlockSpec(memory_space=pltpu.SMEM)
     return pl.pallas_call(
         functools.partial(middle_kernel, seqs, segs, groups, chunks, TOGETHER),
-        in_specs=[smem, smem, anywhere, anywhere, anywhere, vmem],
+        in_specs=[smem, smem, anywhere, anywhere, vmem, anywhere, anywhere, vmem],
         out_specs=vmem,
         out_shape=jax.ShapeDtypeStruct((groups, part_rows, cols), jnp.bfloat16),
         scratch_shapes=[
+            pltpu.VMEM((heads, rows, HD), jnp.bfloat16),
+            pltpu.VMEM(normed.shape, jnp.bfloat16),
+            pltpu.VMEM(w_qkv.shape[1:], jnp.bfloat16),
             pltpu.VMEM((2, seqs * rows // BLOCK, BLOCK, HD), jnp.bfloat16),
             pltpu.VMEM((seqs, part_rows, HD), jnp.bfloat16),
             pltpu.VMEM((seqs, part_rows, HD), jnp.bfloat16),
@@ -365,13 +387,16 @@
             dma((seqs, max(groups - 1, 1))), dma((seqs, max(groups - 1, 1))),
             dma((segs,)), dma((segs,)),
             dma((chunks, seqs)), dma((chunks, seqs)), dma((chunks, 4)), dma((chunks, 4)),
-            dma((3,)), dma((chunks,)),
+            dma((5,)), dma((chunks,)),
         ],
         compiler_params=pltpu.CompilerParams(
             collective_id=0, has_side_effects=True, vmem_limit_bytes=48 * MIB
         ),
         name="middle",
-    )(lists, counts, q, kv.reshape(heads, 2, rows // BLOCK, BLOCK, HD), w_out, share)
+    )(
+        lists, counts, normed, w_qkv, qk_gain,
+        kv.reshape(heads, 2, rows // BLOCK, BLOCK, HD), w_out, share,
+    )
 
 
 def on_device(
@@ -385,9 +410,9 @@
     part_rows = rows // groups
     padded = padded_2(base_latent, "seq", BASE_FT)
     place = (upsample_map - (rank * base_latent.shape[0] - BASE_FT))[:, None]
-    q, kv, share = front(sr_tokens, padded, place, norm_gain[None], w_qkv, qk_gain)
+    normed, kv, share = front(sr_tokens, padded, place, norm_gain[None], w_qkv, qk_gain)
     out = middle(
-        block_lists.reshape(-1), block_counts, q, kv, w_out,
+        block_lists.reshape(-1), block_counts, normed, w_qkv, qk_gain, kv, w_out,
         share.reshape(groups, part_rows, -1), seqs, segs, groups,
     )
     return out.reshape(rows, -1)

time: 152 us -> 149 us (0.980)
  Pallas kernels: 141 us -> 137 us
    pallas_call x1, Pallas kernels: 13.9 us -> 10.5 us  [front(): pl.pallas_call(functools.partial(front_kernel, heads), grid=(rows // tile...]
    unnamed x8 -> x12, local copies, waits for them, and re-layouts: 1.78 us -> 3.11 us
where the time goes in v4:
time: 149 us; the launch traced here: 148 us
  Pallas kernels  137 us (92%)
  starting transfers between devices  3.79 us (3%)
  local copies, waits for them, and re-layouts  3.42 us (2%)
  waiting for transfers between devices  2.7 us (2%)
  other arithmetic  1.71 us (1%)
    pallas_call x1, Pallas kernels, middle(): pl.pallas_call(functools.partial(middle_kernel, seqs, segs, groups, chunk...  126 us
    pallas_call x1, Pallas kernels, front(): pl.pallas_call(functools.partial(front_kernel, heads), grid=(rows // tile...  10.5 us
    unnamed x12, local copies, waits for them, and re-layouts  3.11 us
  transfers between devices with their start and end apart: 2, of which 1 were waited for; matrix products, arithmetic and copies ran while one was open for 1% of the time, Pallas kernels for 0%

profile of v4, /device:TPU:0, one launch (start us, length us, event | category | flops | bytes accessed | tf_op | source)
XLA Modules:
  0.0 148.3 jit_solution(2613431490821455604)
XLA Ops:
  0.0 0.0 copy-start.3
  0.0 0.0 copy-start.2
  0.0 2.5 %collective-permute-start = (bf16[64,2048]{1,0:T(8,128)(2,1)}, bf16[64,2048]{1,0:T(8,128)(2,1)S(1)}, u32[]{:S(2)}, u32[]{:S(2)}) collective-permute-start(bf16[64,2048]{1,0:T(8,128)(2,1)} %param.10), channel_id=1, source_target_pairs={{0,1},{1,2},{2,3},{3,4},{4,5},{5,6},{6,7},{8,9},{9,10},{10,11},{11... | collective-permute-start | bytes 786440 | tf_op jit(solution)/shard_map/ppermute | solution.py:24
  2.5 1.3 collective-permute-start.1
  3.8 0.7 broadcast_subtract_fusion
  4.5 0.2 copy.11.place
  4.7 0.8 copy.10
  5.5 0.1 reshape.12.lists
  5.6 0.0 collective-permute-done
  5.6 2.7 %collective-permute-done.1 = bf16[64,2048]{1,0:T(8,128)(2,1)S(1)} collective-permute-done((bf16[64,2048]{1,0:T(8,128)(2,1)}, bf16[64,2048]{1,0:T(8,128)(2,1)S(1)}, u32[]{:S(2)}, u32[]{:S(2)}) %collective-permute-start.1) | collective-permute-done | bytes 262176 | tf_op jit(solution)/shard_map/ppermute | solution.py:25
  8.3 1.0 pad_maximum_fusion.base
  9.3 0.0 copy-done.3
  9.4 0.0 copy-done.2
  9.4 0.0 copy-start
  9.4 0.0 copy-start.4
  9.4 10.5 %front.1 = (bf16[1024,2048]{1,0:T(8,128)(2,1)}, bf16[4,2,1024,128]{3,2,1,0:T(8,128)(2,1)S(1)}, f32[1024,512]{1,0:T(8,128)S(1)}) custom-call(bf16[1024,2048]{1,0:T(8,128)(2,1)} %sr.1, bf16[192,2048]{1,0:T(8,128)(2,1)S(1)} %pad_maximum_fusion.base, s32[1024,1]{1,0:T(8,128)S(1)} %copy.11.place, f32[1,2048]{1,0:T(1,128)S(1)} %bitcast.8, ...), custom_call_target="tpu_custom_call" | custom-call | tf_op jit(solution)/shard_map/front/pallas_call | solution.py:61
  19.9 0.0 copy-start.1
  19.9 1.3 copy-done.1
  21.2 0.0 copy-done
  21.2 0.0 copy-done.4
  21.2 126.1 %middle.1 = bf16[2,512,512]{2,1,0:T(8,128)(2,1)S(1)} custom-call(s32[1024]{0:T(1024)S(1)} %reshape.12.lists, s32[128]{0:T(128)S(1)} %copy-done.4, bf16[1024,2048]{1,0:T(8,128)(2,1)} %get-tuple-element.8.normed, bf16[3,2048,512]{2,1,0:T(8,128)(2,1)} %w_qkv.3, f32[2,512]{1,0:T(2,128)S(1)} %copy-done.2, bf16[4,2,16,64,128]{4,3,2,1,0:T(8,128)(2,1)S(1)} %bitcast.6, ...), custom_call_target="tpu_custom_call" | custom-call | tf_op jit(solution)/shard_map/middle/pallas_call | solution.py:372
  147.3 1.0 copy.13
Async XLA Ops:
  0.0 9.4 %copy-start.3 = (f32[2048]{0:T(1024)S(1)}, f32[2048]{0:T(1024)}, u32[]{:S(2)}) copy-start(f32[2048]{0:T(1024)} %param.12) | copy-start | bytes 24580
  0.0 9.4 %copy-start.2 = (f32[2,512]{1,0:T(2,128)S(1)}, f32[2,512]{1,0:T(2,128)}, u32[]{:S(2)}) copy-start(f32[2,512]{1,0:T(2,128)} %qk_gain.3) | copy-start | bytes 12292
  0.0 5.6 %collective-permute-start = (bf16[64,2048]{1,0:T(8,128)(2,1)}, bf16[64,2048]{1,0:T(8,128)(2,1)S(1)}, u32[]{:S(2)}, u32[]{:S(2)}) collective-permute-start(bf16[64,2048]{1,0:T(8,128)(2,1)} %param.10), channel_id=1, source_target_pairs={{0,1},{1,2},{2,3},{3,4},{4,5},{5,6},{6,7},{8,9},{9,10},{10,11},{11... | collective-permute-start | bytes 786440 | tf_op jit(solution)/shard_map/ppermute | solution.py:24
  2.5 5.8 %collective-permute-start.1 = (bf16[64,2048]{1,0:T(8,128)(2,1)}, bf16[64,2048]{1,0:T(8,128)(2,1)S(1)}, u32[]{:S(2)}, u32[]{:S(2)}) collective-permute-start(bf16[64,2048]{1,0:T(8,128)(2,1)} %param.10), channel_id=1, source_target_pairs={{1,0},{2,1},{3,2},{4,3},{5,4},{6,5},{7,6},{9,8},{10,9},{11,10},{12... | collective-permute-start | bytes 786440 | tf_op jit(solution)/shard_map/ppermute | solution.py:25
  9.4 11.8 %copy-start = (bf16[512,2048]{1,0:T(8,128)(2,1)S(1)}, bf16[512,2048]{1,0:T(8,128)(2,1)}, u32[]{:S(2)}) copy-start(bf16[512,2048]{1,0:T(8,128)(2,1)} %w_out.1) | copy-start | bytes 6291460
  9.4 11.8 %copy-start.4 = (s32[128]{0:T(128)S(1)}, s32[128]{0:T(128)}, u32[]{:S(2)}) copy-start(s32[128]{0:T(128)} %counts.1) | copy-start | bytes 1540
  19.9 1.3 copy-start.1

commit v5 on v4

--- a/solution.py
+++ b/solution.py
@@ -12,7 +12,7 @@
 BLOCK = 64
 EPSILON = 1e-06
 CHUNKS = 8
-TOGETHER = 4
+TOGETHER = 8
 MESH = pl.DeviceIdType.MESH
 MIB = 2**20
 

time: 149 us -> 147 us (0.987)
  Pallas kernels: 137 us -> 135 us
where the time goes in v5:
time: 147 us
  Pallas kernels  135 us (92%)
  starting transfers between devices  3.79 us (3%)
  local copies, waits for them, and re-layouts  3.42 us (2%)
  waiting for transfers between devices  2.7 us (2%)
  other arithmetic  1.71 us (1%)
    pallas_call x1, Pallas kernels, middle(): pl.pallas_call(functools.partial(middle_kernel, seqs, segs, groups, chunk...  125 us
    pallas_call x1, Pallas kernels, front(): pl.pallas_call(functools.partial(front_kernel, heads), grid=(rows // tile...  10.5 us
    unnamed x12, local copies, waits for them, and re-layouts  3.11 us
  transfers between devices with their start and end apart: 2, of which 1 were waited for; matrix products, arithmetic and copies ran while one was open for 1% of the time, Pallas kernels for 0%

profile of v5, /device:TPU:0, one launch (start us, length us, event | category | flops | bytes accessed | tf_op | source)
XLA Modules:
  0.0 147.0 jit_solution(11804632115534478556)
XLA Ops:
  0.0 0.0 copy-start.3
  0.0 0.0 copy-start.2
  0.0 2.5 %collective-permute-start = (bf16[64,2048]{1,0:T(8,128)(2,1)}, bf16[64,2048]{1,0:T(8,128)(2,1)S(1)}, u32[]{:S(2)}, u32[]{:S(2)}) collective-permute-start(bf16[64,2048]{1,0:T(8,128)(2,1)} %param.10), channel_id=1, source_target_pairs={{0,1},{1,2},{2,3},{3,4},{4,5},{5,6},{6,7},{8,9},{9,10},{10,11},{11... | collective-permute-start | bytes 786440 | tf_op jit(solution)/shard_map/ppermute | solution.py:24
  2.5 1.3 collective-permute-start.1
  3.8 0.7 broadcast_subtract_fusion
  4.5 0.2 copy.11.place
  4.7 0.8 copy.10
  5.5 0.1 reshape.12.lists
  5.6 0.0 collective-permute-done
  5.6 2.7 %collective-permute-done.1 = bf16[64,2048]{1,0:T(8,128)(2,1)S(1)} collective-permute-done((bf16[64,2048]{1,0:T(8,128)(2,1)}, bf16[64,2048]{1,0:T(8,128)(2,1)S(1)}, u32[]{:S(2)}, u32[]{:S(2)}) %collective-permute-start.1) | collective-permute-done | bytes 262176 | tf_op jit(solution)/shard_map/ppermute | solution.py:25
  8.3 1.0 pad_maximum_fusion.base
  9.3 0.0 copy-done.3
  9.4 0.0 copy-done.2
  9.4 0.0 copy-start
  9.4 0.0 copy-start.4
  9.4 10.5 %front.1 = (bf16[1024,2048]{1,0:T(8,128)(2,1)}, bf16[4,2,1024,128]{3,2,1,0:T(8,128)(2,1)S(1)}, f32[1024,512]{1,0:T(8,128)S(1)}) custom-call(bf16[1024,2048]{1,0:T(8,128)(2,1)} %sr.1, bf16[192,2048]{1,0:T(8,128)(2,1)S(1)} %pad_maximum_fusion.base, s32[1024,1]{1,0:T(8,128)S(1)} %copy.11.place, f32[1,2048]{1,0:T(1,128)S(1)} %bitcast.8, ...), custom_call_target="tpu_custom_call" | custom-call | tf_op jit(solution)/shard_map/front/pallas_call | solution.py:61
  19.9 0.0 copy-start.1
  19.9 1.3 copy-done.1
  21.2 0.0 copy-done
  21.2 0.0 copy-done.4
  21.2 124.8 %middle.1 = bf16[2,512,512]{2,1,0:T(8,128)(2,1)S(1)} custom-call(s32[1024]{0:T(1024)S(1)} %reshape.12.lists, s32[128]{0:T(128)S(1)} %copy-done.4, bf16[1024,2048]{1,0:T(8,128)(2,1)} %get-tuple-element.8.normed, bf16[3,2048,512]{2,1,0:T(8,128)(2,1)} %w_qkv.3, f32[2,512]{1,0:T(2,128)S(1)} %copy-done.2, bf16[4,2,16,64,128]{4,3,2,1,0:T(8,128)(2,1)S(1)} %bitcast.6, ...), custom_call_target="tpu_custom_call" | custom-call | tf_op jit(solution)/shard_map/middle/pallas_call | solution.py:372
  146.0 1.0 copy.13
Async XLA Ops:
  0.0 9.4 %copy-start.3 = (f32[2048]{0:T(1024)S(1)}, f32[2048]{0:T(1024)}, u32[]{:S(2)}) copy-start(f32[2048]{0:T(1024)} %param.12) | copy-start | bytes 24580
  0.0 9.4 %copy-start.2 = (f32[2,512]{1,0:T(2,128)S(1)}, f32[2,512]{1,0:T(2,128)}, u32[]{:S(2)}) copy-start(f32[2,512]{1,0:T(2,128)} %qk_gain.3) | copy-start | bytes 12292
  0.0 5.6 %collective-permute-start = (bf16[64,2048]{1,0:T(8,128)(2,1)}, bf16[64,2048]{1,0:T(8,128)(2,1)S(1)}, u32[]{:S(2)}, u32[]{:S(2)}) collective-permute-start(bf16[64,2048]{1,0:T(8,128)(2,1)} %param.10), channel_id=1, source_target_pairs={{0,1},{1,2},{2,3},{3,4},{4,5},{5,6},{6,7},{8,9},{9,10},{10,11},{11... | collective-permute-start | bytes 786440 | tf_op jit(solution)/shard_map/ppermute | solution.py:24
  2.5 5.8 %collective-permute-start.1 = (bf16[64,2048]{1,0:T(8,128)(2,1)}, bf16[64,2048]{1,0:T(8,128)(2,1)S(1)}, u32[]{:S(2)}, u32[]{:S(2)}) collective-permute-start(bf16[64,2048]{1,0:T(8,128)(2,1)} %param.10), channel_id=1, source_target_pairs={{1,0},{2,1},{3,2},{4,3},{5,4},{6,5},{7,6},{9,8},{10,9},{11,10},{12... | collective-permute-start | bytes 786440 | tf_op jit(solution)/shard_map/ppermute | solution.py:25
  9.4 11.8 %copy-start = (bf16[512,2048]{1,0:T(8,128)(2,1)S(1)}, bf16[512,2048]{1,0:T(8,128)(2,1)}, u32[]{:S(2)}) copy-start(bf16[512,2048]{1,0:T(8,128)(2,1)} %w_out.1) | copy-start | bytes 6291460
  9.4 11.8 %copy-start.4 = (s32[128]{0:T(128)S(1)}, s32[128]{0:T(128)}, u32[]{:S(2)}) copy-start(s32[128]{0:T(128)} %counts.1) | copy-start | bytes 1540
  19.9 1.3 copy-start.1
